TPU v7x, 32 devices: a whole 2x2x4 slice. The times are simulated.
32 devices in a mesh: dp: 4 (over y, x), seq: 8 (over z, core).
Axes of the slice: x: 2, y: 2, z: 4, core: 2. Of those that a mesh axis runs over, the one named last changes fastest.
Arguments:
- query_gate: bfloat16 [4, 1024, 4096], P('dp', 'seq'), may hold values from -6 to 6
- key_gate: bfloat16 [4, 1024, 4096], P('dp', 'seq'), may hold values from -6 to 6
- value_feat: bfloat16 [4, 1024, 4096], P('dp', 'seq'), may hold values from -6 to 6
- filters: bfloat16 [256, 128], replicated, may hold values from -0.5 to 0.5
- grad_out: bfloat16 [4, 1024, 4096], P('dp', 'seq'), may hold values from -6 to 6
- basis_prev: float32 [128, 16], replicated, may hold values from -6 to 6
Outputs:
- mixed_out: bfloat16 [4, 1024, 4096], P('dp', 'seq')
- grad_query: bfloat16 [4, 1024, 4096], P('dp', 'seq')
- grad_key: bfloat16 [4, 1024, 4096], P('dp', 'seq')
- grad_value: bfloat16 [4, 1024, 4096], P('dp', 'seq')
- low_rank_grad: float32 [256, 128], replicated
- basis_next: float32 [128, 16], replicated
All inputs are finite; a program needn't handle non-finite values.
Results may differ from a plain program's by a relative error of at most 0.0061.
Values may be sent and summed in bfloat16 or wider, within the bound.
A program may use at most 192 MiB of HBM per device.

v0:
```python
import jax
import jax.numpy as jnp
from jax import lax
from jax.sharding import PartitionSpec as P


def shifted(block, axis, distance):
    devices = range(lax.axis_size(axis))
    route = [(i - distance, i) for i in devices if i - distance in devices]
    return lax.ppermute(block, axis, route)


def orthonormal(left):
    columns = []
    for index in range(left.shape[1]):
        column = left[:, index]
        if index > 0:
            basis = jnp.stack(columns, axis=1)
            coeffs = jnp.dot(basis.T, column, precision=lax.Precision.HIGHEST)
            column = column - jnp.dot(basis, coeffs, precision=lax.Precision.HIGHEST)
        columns.append(column / jnp.sqrt(jnp.sum(column * column) + 1e-06))
    return jnp.stack(columns, axis=1)


def banded(vec, rows):
    count, taps = vec.shape
    width = rows + taps - 1
    line = jnp.concatenate([vec, jnp.zeros((count, rows), vec.dtype)], axis=1)
    tiled = jnp.tile(line, (1, rows))[:, : rows * width]
    return tiled.reshape(count, rows, width)


def lag_sums(cross, taps):
    count, rows, width = cross.shape
    flat = cross.reshape(count, rows * width)[:, : (rows - 1) * 2 * taps]
    upper = flat.reshape(count, rows - 1, 2 * taps)[:, :, :taps].sum(axis=1)
    return upper + cross[:, rows - 1, rows - 1 : rows - 1 + taps]


def on_device(query_gate, key_gate, value_feat, filters, grad_out, basis_prev):
    gate_q = query_gate[0].astype(jnp.float32)
    gate_k = key_gate[0].astype(jnp.float32)
    feat_v = value_feat[0].astype(jnp.float32)
    cotan = grad_out[0].astype(jnp.float32)
    tok, channels = gate_q.shape
    groups, taps = filters.shape
    group_size = channels // groups
    width = tok + taps - 1
    product = (gate_k * feat_v).astype(jnp.bfloat16)
    grad_conv = (cotan * gate_q).astype(jnp.bfloat16)
    before = shifted(product[tok - (taps - 1) :], "seq", 1)
    after = shifted(grad_conv[: taps - 1], "seq", -1)
    prod_cm = jnp.concatenate([before, product], axis=0).T.reshape(groups, group_size, width)
    grad_cm = jnp.concatenate([grad_conv, after], axis=0).T.reshape(groups, group_size, width)
    block_groups = min(64, groups)
    conv_parts = []
    back_parts = []
    filter_parts = []
    for block in range(groups // block_groups):
        low = block * block_groups
        filt_blk = filters[low : low + block_groups]
        forward_tab = banded(filt_blk[:, ::-1], taps)
        backward_tab = banded(filt_blk, taps)
        prod_blk = prod_cm[low : low + block_groups]
        grad_blk = grad_cm[low : low + block_groups]
        conv_pos = jnp.einsum(
            "gcu,gsu->gcs", prod_blk, forward_tab, preferred_element_type=jnp.float32
        )
        back_pos = jnp.einsum(
            "gcu,gsu->gcs", grad_blk, backward_tab, preferred_element_type=jnp.float32
        )
        cross = jnp.einsum(
            "gcs,gcu->gsu", grad_blk[:, :, :taps], prod_blk, preferred_element_type=jnp.float32
        )
        lag_total = lag_sums(cross, taps)
        conv_parts.append(conv_pos)
        back_parts.append(back_pos)
        filter_parts.append(lag_total[:, ::-1])
    conv = jnp.concatenate(conv_parts, axis=0).reshape(channels, tok).T
    grad_product = jnp.concatenate(back_parts, axis=0).reshape(channels, tok).T
    local_grad = jnp.concatenate(filter_parts, axis=0)
    mixed_out = (gate_q * conv).astype(jnp.bfloat16)[None]
    grad_query = (cotan * conv).astype(jnp.bfloat16)[None]
    grad_key = (grad_product * feat_v).astype(jnp.bfloat16)[None]
    grad_value = (grad_product * gate_k).astype(jnp.bfloat16)[None]
    scale = (lax.axis_size("dp") * lax.axis_size("seq") * tok * group_size) ** (-0.5)
    seq_grad = lax.psum(local_grad, "seq")
    left = lax.psum(jnp.dot(seq_grad, basis_prev, precision=lax.Precision.HIGHEST), "dp")
    ortho = orthonormal(left)
    right = lax.psum(jnp.dot(seq_grad.T, ortho, precision=lax.Precision.HIGHEST), "dp")
    basis_next = right * scale
    low_rank_grad = jnp.dot(ortho, basis_next.T, precision=lax.Precision.HIGHEST)
    return (mixed_out, grad_query, grad_key, grad_value, low_rank_grad, basis_next)


def solution(mesh):
    return jax.shard_map(
        on_device,
        mesh=mesh,
        in_specs=(
            P("dp", "seq", None),
            P("dp", "seq", None),
            P("dp", "seq", None),
            P(),
            P("dp", "seq", None),
            P(),
        ),
        out_specs=(
            P("dp", "seq", None),
            P("dp", "seq", None),
            P("dp", "seq", None),
            P("dp", "seq", None),
            P(),
            P(),
        ),
        check_vma=False,
    )
```

profile of v0, /device:TPU:0, one launch (start us, length us, event | category | flops | bytes accessed | tf_op | source)
XLA Modules:
  0.0 459.0 jit_solution(2387971352941314177)
XLA Ops:
  16.3 16.0 %reshape.134 = bf16[64,128,255]{2,1,0:T(8,128)(2,1)} reshape(bf16[64,32640]{1,0:T(8,128)(2,1)} %slice.263) | data formatting | bytes 8355840 | tf_op jit(solution)/shard_map/reshape | solution.py:30
  37.4 15.8 %reshape.135 = bf16[64,128,255]{2,1,0:T(8,128)(2,1)} reshape(bf16[64,32640]{1,0:T(8,128)(2,1)} %slice.265) | data formatting | bytes 8355840 | tf_op jit(solution)/shard_map/reshape | solution.py:30
  58.3 16.2 %reshape.133 = bf16[64,128,255]{2,1,0:T(8,128)(2,1)} reshape(bf16[64,32640]{1,0:T(8,128)(2,1)} %slice.261) | data formatting | bytes 8355840 | tf_op jit(solution)/shard_map/reshape | solution.py:30
  79.5 15.8 %reshape.132 = bf16[64,128,255]{2,1,0:T(8,128)(2,1)} reshape(bf16[64,32640]{1,0:T(8,128)(2,1)} %slice.259) | data formatting | bytes 8355840 | tf_op jit(solution)/shard_map/reshape | solution.py:30
  96.6 3.6 fusion.64
  107.7 3.6 fusion.6
  111.5 4.0 collective-permute-start
  121.0 15.8 %reshape.129 = bf16[64,128,255]{2,1,0:T(8,128)(2,1)} reshape(bf16[64,32640]{1,0:T(8,128)(2,1)} %slice.254) | data formatting | bytes 8355840 | tf_op jit(solution)/shard_map/reshape | solution.py:30
  141.9 15.8 %reshape.130 = bf16[64,128,255]{2,1,0:T(8,128)(2,1)} reshape(bf16[64,32640]{1,0:T(8,128)(2,1)} %slice.256) | data formatting | bytes 8355840 | tf_op jit(solution)/shard_map/reshape | solution.py:30
  162.8 16.2 %reshape.128 = bf16[64,128,255]{2,1,0:T(8,128)(2,1)} reshape(bf16[64,32640]{1,0:T(8,128)(2,1)} %slice.252) | data formatting | bytes 8355840 | tf_op jit(solution)/shard_map/reshape | solution.py:30
  184.1 15.8 %reshape.127 = bf16[64,128,255]{2,1,0:T(8,128)(2,1)} reshape(bf16[64,32640]{1,0:T(8,128)(2,1)} %slice.250) | data formatting | bytes 8355840 | tf_op jit(solution)/shard_map/reshape | solution.py:30
  203.3 3.2 copy-done.1
  206.6 9.4 %reshape.139 = f32[64,32640]{1,0:T(8,128)} reshape(f32[64,128,255]{2,1,0:T(8,128)} %copy-done.1) | data formatting | bytes 16711680 | tf_op jit(solution)/shard_map/reshape | solution.py:35
  217.6 3.2 copy-done.2
  221.0 9.3 %reshape.141 = f32[64,32640]{1,0:T(8,128)} reshape(f32[64,128,255]{2,1,0:T(8,128)} %copy-done.2) | data formatting | bytes 16711680 | tf_op jit(solution)/shard_map/reshape | solution.py:35
  231.8 3.2 copy-done.3
  235.1 9.3 %reshape.143 = f32[64,32640]{1,0:T(8,128)} reshape(f32[64,128,255]{2,1,0:T(8,128)} %copy-done.3) | data formatting | bytes 16711680 | tf_op jit(solution)/shard_map/reshape | solution.py:35
  246.0 3.2 copy-done.4
  249.3 9.3 %reshape.137 = f32[64,32640]{1,0:T(8,128)} reshape(f32[64,128,255]{2,1,0:T(8,128)} %copy-done.4) | data formatting | bytes 16711680 | tf_op jit(solution)/shard_map/reshape | solution.py:35
  258.6 3.5 fusion.58
  262.1 3.5 fusion.61
  271.5 7.1 %slice.271 = f32[64,32512]{1,0:T(8,128)} slice(f32[64,32640]{1,0:T(8,128)} %reshape.139), slice={[0:64], [0:32512]} | slice | bytes 16646144 | tf_op jit(solution)/shard_map/slice | solution.py:35
  278.6 7.6 %reshape.140 = f32[64,127,256]{2,1,0:T(8,128)} reshape(f32[64,32512]{1,0:T(8,128)} %slice.271) | data formatting | bytes 16646144 | tf_op jit(solution)/shard_map/reshape | solution.py:36
  289.0 7.1 %slice.275 = f32[64,32512]{1,0:T(8,128)} slice(f32[64,32640]{1,0:T(8,128)} %reshape.141), slice={[0:64], [0:32512]} | slice | bytes 16646144 | tf_op jit(solution)/shard_map/slice | solution.py:35
  296.0 7.4 %reshape.142 = f32[64,127,256]{2,1,0:T(8,128)} reshape(f32[64,32512]{1,0:T(8,128)} %slice.275) | data formatting | bytes 16646144 | tf_op jit(solution)/shard_map/reshape | solution.py:36
  306.2 7.1 %slice.279 = f32[64,32512]{1,0:T(8,128)} slice(f32[64,32640]{1,0:T(8,128)} %reshape.143), slice={[0:64], [0:32512]} | slice | bytes 16646144 | tf_op jit(solution)/shard_map/slice | solution.py:35
  313.3 7.4 %reshape.144 = f32[64,127,256]{2,1,0:T(8,128)} reshape(f32[64,32512]{1,0:T(8,128)} %slice.279) | data formatting | bytes 16646144 | tf_op jit(solution)/shard_map/reshape | solution.py:36
  323.5 7.1 %slice.267 = f32[64,32512]{1,0:T(8,128)} slice(f32[64,32640]{1,0:T(8,128)} %reshape.137), slice={[0:64], [0:32512]} | slice | bytes 16646144 | tf_op jit(solution)/shard_map/slice | solution.py:35
  330.6 7.4 %reshape.138 = f32[64,127,256]{2,1,0:T(8,128)} reshape(f32[64,32512]{1,0:T(8,128)} %slice.267) | data formatting | bytes 16646144 | tf_op jit(solution)/shard_map/reshape | solution.py:36
  344.6 53.1 %all-reduce.10.cloned.1.call-done = f32[256,128]{1,0:T(8,128)} async-done(((f32[256,128]{1,0:T(8,128)}), f32[256,128]{1,0:T(8,128)}) %all-reduce.10.cloned.1.call-update) | async-done | bytes 131088 | tf_op jit(solution)/shard_map/psum | solution.py:87
  398.8 16.0 %psum.22 = f32[256,16]{0,1:T(8,128)S(1)} all-reduce(f32[256,16]{0,1:T(8,128)S(1)} %fusion.66), channel_id=1, replica_groups=mesh['dp'=4,'seq'=8] {'dp'}, use_global_device_ids=true, to_apply=%region_5.0 | all-reduce | flops 4096 | bytes 32768 | tf_op jit(solution)/shard_map/psum | solution.py:88
  443.3 7.6 %psum.23 = f32[128,16]{0,1:T(8,128)S(1)} all-reduce(f32[128,16]{0,1:T(8,128)S(1)} %fusion.78), channel_id=1, replica_groups=mesh['dp'=4,'seq'=8] {'dp'}, use_global_device_ids=true, to_apply=%region_22.0 | all-reduce | flops 2048 | bytes 16384 | tf_op jit(solution)/shard_map/psum | solution.py:90
  (200 shorter events, 101.9 us)
Async XLA Ops:
  7.2 390.5 %copy-start = (f32[128,16]{0,1:T(8,128)S(1)}, f32[128,16]{0,1:T(8,128)}, u32[]{:S(2)}) copy-start(f32[128,16]{0,1:T(8,128)} %param.11) | copy-start | bytes 24580
  7.2 390.5 %all-reduce.10.cloned.1.call-start = ((), (), s32[]{:S(2)}) async-start(), calls=%async_computation | async-start | bytes 262144 | tf_op jit(solution)/shard_map/psum | solution.py:87
  9.0 86.3 %collective-permute-start.1 = (bf16[127,4096]{1,0:T(8,128)(2,1)S(1)}, bf16[127,4096]{1,0:T(8,128)(2,1)S(1)}, u32[]{:S(2)}, u32[]{:S(2)}) collective-permute-start(bf16[127,4096]{1,0:T(8,128)(2,1)S(1)} %bitcast.286), channel_id=1, source_target_pairs={{1,0},{2,1},{3,2},{4,3},{5,4},{6,5},{7,6},{9,8},{10,9},{11,10},{12... | collective-permute-start | bytes 3121160 | tf_op jit(solution)/shard_map/ppermute | solution.py:10
  95.9 6.7 %copy-start.11 = (bf16[1024,255]{1,0:T(8,128)(2,1)}, bf16[1024,255]{1,0:T(8,128)(2,1)S(1)}, u32[]{:S(2)}) copy-start(bf16[1024,255]{1,0:T(8,128)(2,1)S(1)} %copy.30) | copy-start | bytes 1566724
  96.1 5.3 %copy-start.13 = (bf16[1024,255]{1,0:T(8,128)(2,1)}, bf16[1024,255]{1,0:T(8,128)(2,1)S(1)}, u32[]{:S(2)}) copy-start(bf16[1024,255]{1,0:T(8,128)(2,1)S(1)} %copy.33) | copy-start | bytes 1566724
  96.4 5.1 %copy-start.15 = (bf16[1024,255]{1,0:T(8,128)(2,1)}, bf16[1024,255]{1,0:T(8,128)(2,1)S(1)}, u32[]{:S(2)}) copy-start(bf16[1024,255]{1,0:T(8,128)(2,1)S(1)} %copy.32) | copy-start | bytes 1566724
  96.6 4.9 %copy-start.17 = (bf16[1024,255]{1,0:T(8,128)(2,1)}, bf16[1024,255]{1,0:T(8,128)(2,1)S(1)}, u32[]{:S(2)}) copy-start(bf16[1024,255]{1,0:T(8,128)(2,1)S(1)} %copy.31) | copy-start | bytes 1566724
  96.6 3.6 copy-start.7
  96.6 4.9 %copy-start.8 = (bf16[64,128,255]{2,1,0:T(8,128)(2,1)S(1)}, bf16[64,128,255]{2,1,0:T(8,128)(2,1)}, u32[]{:S(2)}) copy-start(bf16[64,128,255]{2,1,0:T(8,128)(2,1)} %reshape.133) | copy-start | bytes 12533764
  100.2 2.7 copy-start.9
  111.5 88.4 %collective-permute-start = (bf16[127,4096]{1,0:T(8,128)(2,1)S(1)}, bf16[127,4096]{1,0:T(8,128)(2,1)}, u32[]{:S(2)}, u32[]{:S(2)}) collective-permute-start(bf16[127,4096]{1,0:T(8,128)(2,1)S(1)} %slice.248), channel_id=1, source_target_pairs={{0,1},{1,2},{2,3},{3,4},{4,5},{5,6},{6,7},{8,9},{9,10},{10,11},{11... | collective-permute-start | bytes 3121160 | tf_op jit(solution)/shard_map/ppermute | solution.py:10
  199.9 2.0 copy-start.18
  203.3 3.2 copy-start.1
  206.6 9.6 %copy-start.16 = (bf16[1024,255]{1,0:T(8,128)(2,1)S(1)}, bf16[1024,255]{1,0:T(8,128)(2,1)}, u32[]{:S(2)}) copy-start(bf16[1024,255]{1,0:T(8,128)(2,1)} %copy-done.15) | copy-start | bytes 1566724
  217.6 3.2 copy-start.2
  220.9 9.5 %copy-start.14 = (bf16[1024,255]{1,0:T(8,128)(2,1)S(1)}, bf16[1024,255]{1,0:T(8,128)(2,1)}, u32[]{:S(2)}) copy-start(bf16[1024,255]{1,0:T(8,128)(2,1)} %copy-done.13) | copy-start | bytes 1566724
  231.8 3.2 copy-start.3
  235.1 9.5 %copy-start.12 = (bf16[1024,255]{1,0:T(8,128)(2,1)S(1)}, bf16[1024,255]{1,0:T(8,128)(2,1)}, u32[]{:S(2)}) copy-start(bf16[1024,255]{1,0:T(8,128)(2,1)} %copy-done.11) | copy-start | bytes 1566724
  246.0 3.2 copy-start.4
  258.6 7.1 %copy-start.5 = (bf16[64,128,255]{2,1,0:T(8,128)(2,1)S(1)}, bf16[64,128,255]{2,1,0:T(8,128)(2,1)}, u32[]{:S(2)}) copy-start(bf16[64,128,255]{2,1,0:T(8,128)(2,1)} %reshape.129) | copy-start | bytes 12533764
  262.1 4.8 %copy-start.6 = (bf16[64,128,255]{2,1,0:T(8,128)(2,1)S(1)}, bf16[64,128,255]{2,1,0:T(8,128)(2,1)}, u32[]{:S(2)}) copy-start(bf16[64,128,255]{2,1,0:T(8,128)(2,1)} %reshape.128) | copy-start | bytes 12533764
  338.0 3.5 copy-start.10
  450.9 1.1 copy-start.19
Sparse Core Ops, SparseCore 0:
  341.7 56.0 all-reduce.9
where the time goes:
time: 464 us; the launch traced here: 459 us
  local copies, waits for them, and re-layouts  286 us (62%)
  waiting for transfers between devices  53.1 us (11%)
  other arithmetic  36.3 us (8%)
  matrix products  28.7 us (6%)
  between operations  26.1 us (6%)
  blocking collectives  23.6 us (5%)
  starting transfers between devices  5.35 us (1%)
    reshape x8, local copies, waits for them, and re-layouts, banded(): return tiled.reshape(count, rows, width)  128 us
    psum x1, waiting for transfers between devices, on_device(): seq_grad = lax.psum(local_grad, 'seq')  53.1 us
    reshape x4, local copies, waits for them, and re-layouts, lag_sums(): flat = cross.reshape(count, rows * width)[:, :(rows - 1) * 2 * taps]  37.3 us
    unnamed x48, local copies, waits for them, and re-layouts  33.8 us
    reshape x4, local copies, waits for them, and re-layouts, lag_sums(): upper = flat.reshape(count, rows - 1, 2 * taps)[:, :, :taps].sum(axis=1)  29.9 us
    slice x4, local copies, waits for them, and re-layouts, lag_sums(): flat = cross.reshape(count, rows * width)[:, :(rows - 1) * 2 * taps]  28.4 us
    slice x8, local copies, waits for them, and re-layouts, banded(): tiled = jnp.tile(line, (1, rows))[:, :rows * width]  17.7 us
    psum x1, blocking collectives, on_device(): lax.psum(jnp.dot(seq_grad, basis_prev, precision=lax.Precision.HIGHEST),...  16 us
  transfers between devices with their start and end apart: 3, of which 1 were waited for; matrix products, arithmetic and copies ran while one was open for 38% of the time, Pallas kernels for 0%

commit v1 on v0

v1 whole, which is shorter than its diff:
```python
import functools

import jax
import jax.numpy as jnp
from jax import lax
from jax.experimental import pallas as pl
from jax.experimental.pallas import tpu as pltpu
from jax.sharding import PartitionSpec as P

MESH = pl.DeviceIdType.MESH
HIGHEST = lax.Precision.HIGHEST
F32 = jnp.float32
BF16 = jnp.bfloat16
STEP = 32
LANES = 128


def flipped(size, dtype):
    rows = lax.broadcasted_iota(jnp.int32, (size, size), 0)
    cols = lax.broadcasted_iota(jnp.int32, (size, size), 1)
    return jnp.where(rows + cols == size - 1, 1.0, 0.0).astype(dtype)


def gated(left, right):
    return (left.astype(F32) * right.astype(F32)).astype(BF16)


def halo_kernel(chunks, q, k, v, g, prod_halo, grad_halo, prod, grad, send_p, recv_p, send_g, recv_g):
    me = lax.axis_index("seq")
    last = lax.axis_size("seq") - 1
    tok, channels = q.shape
    width = channels // chunks

    barrier = pltpu.get_barrier_semaphore()

    @pl.when(me > 0)
    def _():
        pl.semaphore_signal(barrier, inc=1, device_id={"seq": me - 1}, device_id_type=MESH)

    @pl.when(me < last)
    def _():
        pl.semaphore_signal(barrier, inc=1, device_id={"seq": me + 1}, device_id_type=MESH)

    def to_next(c):
        lanes = pl.ds(c * width, width)
        return pltpu.make_async_remote_copy(
            src_ref=prod.at[:, lanes], dst_ref=prod_halo.at[:, lanes], send_sem=send_p.at[c],
            recv_sem=recv_p.at[c], device_id={"seq": me + 1}, device_id_type=MESH)

    def to_previous(c):
        lanes = pl.ds(c * width, width)
        return pltpu.make_async_remote_copy(
            src_ref=grad.at[:, lanes], dst_ref=grad_halo.at[:, lanes], send_sem=send_g.at[c],
            recv_sem=recv_g.at[c], device_id={"seq": me - 1}, device_id_type=MESH)

    flip = flipped(tok, BF16)
    for c in range(chunks):
        lanes = pl.ds(c * width, width)
        prod[:, lanes] = gated(k[:, lanes], v[:, lanes])
        grad[:, lanes] = jnp.dot(
            flip, gated(g[:, lanes], q[:, lanes]), preferred_element_type=F32).astype(BF16)
        if c == 0:
            pl.semaphore_wait(barrier, (me > 0).astype(jnp.int32) + (me < last).astype(jnp.int32))

        @pl.when(me < last)
        def _():
            to_next(c).start()

        @pl.when(me > 0)
        def _():
            to_previous(c).start()

    for c in range(chunks):
        @pl.when(me < last)
        def _():
            to_next(c).wait_send()
            to_previous(c).wait_recv()

        @pl.when(me > 0)
        def _():
            to_previous(c).wait_send()
            to_next(c).wait_recv()


def mixer_kernel(group, q, k, v, g, prod_halo, grad_halo, lines, mixed, grad_q, grad_k, grad_v, lag, ext):
    me = lax.axis_index("seq")
    last = lax.axis_size("seq") - 1
    tok, width = q.shape
    subs = width // LANES
    per = LANES // group
    blocks = tok // STEP
    rows = 2 * tok
    flip = flipped(tok, BF16)
    prod = gated(k[...], v[...])
    grad = jnp.dot(flip, gated(g[...], q[...]), preferred_element_type=F32).astype(BF16)
    before = jnp.where(me > 0, prod_halo[...], jnp.zeros_like(prod))
    after = jnp.where(me < last, grad_halo[...], jnp.zeros_like(grad))
    for s in range(subs):
        lanes = slice(s * LANES, (s + 1) * LANES)
        low = slice(2 * s * LANES, (2 * s + 1) * LANES)
        high = slice((2 * s + 1) * LANES, (2 * s + 2) * LANES)
        ext[0:tok, low] = before[:, lanes]
        ext[tok:rows, low] = prod[:, lanes]
        ext[0:tok, high] = after[:, lanes]
        ext[tok:rows, high] = grad[:, lanes]
    ext[rows:, :] = jnp.zeros((ext.shape[0] - rows, ext.shape[1]), BF16)
    owner = lax.broadcasted_iota(jnp.int32, (STEP, 2 * LANES), 1) % LANES // group
    flip2 = jnp.concatenate([flip, flip], axis=1)
    for s in range(subs):
        lanes = slice(s * LANES, (s + 1) * LANES)
        low = slice(2 * s * LANES, (2 * s + 1) * LANES)
        high = slice((2 * s + 1) * LANES, (2 * s + 2) * LANES)
        both = slice(2 * s * LANES, (2 * s + 2) * LANES)
        band = jnp.concatenate(
            [
                pltpu.roll(
                    jnp.broadcast_to(lines[s * per + i : s * per + i + 1, :], (STEP, rows)),
                    0, axis=1, stride=1, stride_axis=0,
                ).astype(BF16)
                for i in range(per)
            ],
            axis=0,
        )
        cross = jnp.zeros((per * STEP, rows), F32)
        for pair in range(0, blocks, 2):
            one, two = pair, pair + 1
            at_one = tok + STEP * (blocks - 1 - one)
            at_two = tok + STEP * (blocks - 1 - two)
            cot = jnp.concatenate([ext[at_one : at_one + STEP, high], ext[at_two : at_two + STEP, high]], axis=1)
            windows = jnp.concatenate(
                [ext[STEP * one : STEP * one + rows, low], ext[STEP * two : STEP * two + rows, low]], axis=1)
            masked = jnp.concatenate(
                [jnp.where(owner == i, cot, jnp.zeros_like(cot)) for i in range(per)], axis=0)
            cross = cross + lax.dot_general(
                masked, windows, (((1,), (1,)), ((), ())), preferred_element_type=F32)
        sums = []
        for i in range(per):
            skewed = pltpu.roll(
                cross[i * STEP : (i + 1) * STEP, :], rows - STEP, axis=1, stride=1, stride_axis=0)
            sums.append(jnp.sum(skewed, axis=0, keepdims=True)[:, :tok])
        lag[s * per : (s + 1) * per, :] = jnp.concatenate(sums, axis=0)
        parts = []
        for a in range(blocks):
            res = jnp.dot(band, ext[STEP * a : STEP * a + rows, both], preferred_element_type=F32)
            out = res[0:STEP, :]
            for i in range(1, per):
                out = jnp.where(owner == i, res[i * STEP : (i + 1) * STEP, :], out)
            parts.append(out)
        whole = jnp.concatenate(parts, axis=0)
        conv = whole[:, :LANES]
        back = whole[:, LANES:]
        coarse = back.astype(BF16)
        fine = (back - coarse.astype(F32)).astype(BF16)
        grad_prod = jnp.dot(flip2, jnp.concatenate([coarse, fine], axis=0), preferred_element_type=F32)
        mixed[:, lanes] = (q[:, lanes].astype(F32) * conv).astype(BF16)
        grad_q[:, lanes] = (g[:, lanes].astype(F32) * conv).astype(BF16)
        grad_k[:, lanes] = (grad_prod * v[:, lanes].astype(F32)).astype(BF16)
        grad_v[:, lanes] = (grad_prod * k[:, lanes].astype(F32)).astype(BF16)


def factor_kernel(scale, lag, basis, low_rank, basis_next, parts, mine, gathered, send_a, recv_a, send_b, recv_b):
    dp, seq = lax.axis_size("dp"), lax.axis_size("seq")
    count = dp * seq
    me = lax.axis_index("dp") * seq + lax.axis_index("seq")
    rows = lag.shape[1]

    def where(k):
        peer = lax.rem(me + k, count)
        return peer, (peer // seq, lax.rem(peer, seq))

    barrier = pltpu.get_barrier_semaphore()

    @pl.loop(1, count)
    def _(k):
        pl.semaphore_signal(barrier, inc=1, device_id=where(k)[1], device_id_type=MESH)

    pl.semaphore_wait(barrier, count - 1)

    def scatter(k):
        peer, place = where(k)
        return pltpu.make_async_remote_copy(
            src_ref=lag.at[peer], dst_ref=parts.at[k], send_sem=send_a.at[k],
            recv_sem=recv_a.at[k], device_id=place, device_id_type=MESH)

    def gather(k):
        peer, place = where(k)
        return pltpu.make_async_remote_copy(
            src_ref=mine, dst_ref=gathered.at[me], send_sem=send_b.at[k],
            recv_sem=recv_b.at[k], device_id=place, device_id_type=MESH)

    @pl.loop(1, count)
    def _(k):
        scatter(k).start()

    parts[0] = lag[me]

    @pl.loop(1, count)
    def _(k):
        scatter(k).wait_recv()

    mine[...] = jnp.sum(parts[...], axis=0)

    @pl.loop(1, count)
    def _(k):
        gather(k).start()

    gathered[me] = mine[...]

    @pl.loop(1, count)
    def _(k):
        peer = lax.rem(me + count - k, count)
        pltpu.make_async_remote_copy(
            src_ref=mine, dst_ref=gathered.at[peer], send_sem=send_b.at[k],
            recv_sem=recv_b.at[k], device_id=where(k)[1], device_id_type=MESH).wait_recv()

    grads = gathered[...].reshape(count * rows, lag.shape[2])
    contract = (((1,), (1,)), ((), ()))
    left = lax.dot_general(basis[...], grads, contract, precision=HIGHEST, preferred_element_type=F32)
    rank = left.shape[0]
    index = lax.broadcasted_iota(jnp.int32, left.shape, 0)
    rest = left
    ortho = jnp.zeros_like(left)
    for i in range(rank):
        column = rest[i : i + 1, :]
        norm = jnp.sum(column * column, axis=1, keepdims=True) + 1e-06
        along = jnp.sum(left * column, axis=1, keepdims=True)
        ortho = jnp.where(index == i, column / jnp.sqrt(norm), ortho)
        rest = rest - (along / norm) * column
    right = jnp.dot(ortho, grads, precision=HIGHEST, preferred_element_type=F32) * scale
    flip = flipped(lag.shape[2], F32)
    basis_next[...] = lax.dot_general(flip, right, contract, precision=HIGHEST, preferred_element_type=F32)
    right = jnp.dot(right, flip, precision=HIGHEST, preferred_element_type=F32)
    low_rank[...] = lax.dot_general(
        ortho, right, (((0,), (0,)), ((), ())), precision=HIGHEST, preferred_element_type=F32)

    @pl.loop(1, count)
    def _(k):
        scatter(k).wait_send()
        gather(k).wait_send()


def on_device(query_gate, key_gate, value_feat, filters, grad_out, basis_prev):
    q, k, v, g = query_gate[0], key_gate[0], value_feat[0], grad_out[0]
    tok, channels = q.shape
    groups, taps = filters.shape
    group = channels // groups
    count = lax.axis_size("dp") * lax.axis_size("seq")
    rank = basis_prev.shape[1]
    vmem = pl.BlockSpec(memory_space=pltpu.VMEM)
    anywhere = pl.BlockSpec(memory_space=pl.ANY)
    block = jax.ShapeDtypeStruct((tok, channels), BF16)

    chunks = 8
    prod_halo, grad_halo = pl.pallas_call(
        functools.partial(halo_kernel, chunks),
        out_shape=(block, block),
        in_specs=[vmem] * 4,
        out_specs=(anywhere, anywhere),
        scratch_shapes=[pltpu.VMEM((tok, channels), BF16)] * 2 + [pltpu.SemaphoreType.DMA((chunks,))] * 4,
        compiler_params=pltpu.CompilerParams(
            collective_id=0, has_side_effects=True, vmem_limit_bytes=48 * 2**20),
        name="halo",
    )(q, k, v, g)

    line = jnp.pad(filters[:, ::-1].astype(F32), ((0, 0), (1, 2 * tok - taps - 1)))
    width = 512
    wide = pl.BlockSpec((tok, width), lambda i: (0, i))
    mixed, grad_q, grad_k, grad_v, lag = pl.pallas_call(
        functools.partial(mixer_kernel, group),
        grid=(channels // width,),
        out_shape=(block,) * 4 + (jax.ShapeDtypeStruct((groups, taps), F32),),
        in_specs=[wide] * 6 + [pl.BlockSpec((width // group, 2 * tok), lambda i: (i, 0))],
        out_specs=[wide] * 4 + [pl.BlockSpec((width // group, taps), lambda i: (i, 0))],
        scratch_shapes=[pltpu.VMEM((3 * tok - STEP, 2 * width), BF16)],
        compiler_params=pltpu.CompilerParams(vmem_limit_bytes=48 * 2**20),
        name="mixer",
    )(q, k, v, g, prod_halo, grad_halo, line)

    scale = (lax.axis_size("dp") * lax.axis_size("seq") * tok * group) ** (-0.5)
    rows = groups // count
    low_rank, basis_next = pl.pallas_call(
        functools.partial(factor_kernel, scale),
        out_shape=(
            jax.ShapeDtypeStruct((groups, taps), F32),
            jax.ShapeDtypeStruct((taps, rank), F32),
        ),
        in_specs=[vmem] * 2,
        out_specs=(vmem, vmem),
        scratch_shapes=[
            pltpu.VMEM((count, rows, taps), F32),
            pltpu.VMEM((rows, taps), F32),
            pltpu.VMEM((count, rows, taps), F32),
        ] + [pltpu.SemaphoreType.DMA((count,))] * 4,
        compiler_params=pltpu.CompilerParams(
            collective_id=1, has_side_effects=True, vmem_limit_bytes=16 * 2**20),
        name="factors",
    )(lag.reshape(count, rows, taps), basis_prev[::-1].T)
    return (mixed[None], grad_q[None], grad_k[None], grad_v[None], low_rank, basis_next)


def solution(mesh):
    spec = P("dp", "seq", None)
    return jax.shard_map(
        on_device,
        mesh=mesh,
        in_specs=(spec, spec, spec, P(), spec, P()),
        out_specs=(spec, spec, spec, spec, P(), P()),
        check_vma=False,
    )
```

time: 464 us -> 64.6 us (0.14); the launches traced: 459 us -> 64.3 us
  local copies, waits for them, and re-layouts: 286 us -> 9.67 us
  Pallas kernels: 0 us -> 53.8 us
  waiting for transfers between devices: 53.1 us -> 0 us
  other arithmetic: 36.3 us -> 0.1 us
  matrix products: 28.7 us -> 0 us
  between operations: 26.1 us -> 0.73 us
  blocking collectives: 23.6 us -> 0 us
  starting transfers between devices: 5.35 us -> 0 us
    reshape x18 -> x0, local copies, waits for them, and re-layouts: 199 us -> none  [the longest x8 128 us: banded(): return tiled.reshape(count, rows, width)]
    pallas_call x0 -> x3, Pallas kernels: none -> 53.8 us  [the longest x1 30.1 us: on_device(): pl.pallas_call(functools.partial(factor_kernel, scale), out_shape=(jax.Sh...]
    psum x1 -> x0, waiting for transfers between devices: 53.1 us -> none  [on_device(): seq_grad = lax.psum(local_grad, 'seq')]
    slice x28 -> x0, local copies, waits for them, and re-layouts: 49.7 us -> none  [the longest x4 28.4 us: lag_sums(): flat = cross.reshape(count, rows * width)[:, :(rows - 1) * 2 * taps]]
    dot_general x43 -> x0, matrix products: 28.7 us -> none  [the longest x4 9.46 us: on_device(): jnp.einsum('gcu,gsu->gcs', prod_blk, forward_tab, preferred_element_type=...]
    unnamed x48 -> x26, local copies, waits for them, and re-layouts: 33.8 us -> 9.4 us
    psum x2 -> x0, blocking collectives: 23.6 us -> none  [the longest x1 16 us: on_device(): lax.psum(jnp.dot(seq_grad, basis_prev, precision=lax.Precision.HIGHEST),...]
    reduce_sum x20 -> x0, other arithmetic: 21.1 us -> none  [the longest x4 10.6 us: lag_sums(): upper = flat.reshape(count, rows - 1, 2 * taps)[:, :, :taps].sum(axis=1)]
  transfers between devices with their start and end apart: 3 -> 0, of which waited for: 1 -> 0; matrix products, arithmetic and copies ran while one was open for 38% -> 0% of each run, Pallas kernels for 0% -> 0%
where the time goes in v1:
time: 64.6 us; the launch traced here: 64.3 us
  Pallas kernels  53.8 us (83%)
  local copies, waits for them, and re-layouts  9.67 us (15%)
  between operations  0.73 us (1%)
    pallas_call x1, Pallas kernels, on_device(): pl.pallas_call(functools.partial(factor_kernel, scale), out_shape=(jax.Sh...  30.1 us
    pallas_call x1, Pallas kernels, on_device(): pl.pallas_call(functools.partial(mixer_kernel, group), grid=(channels //...  16.3 us
    unnamed x26, local copies, waits for them, and re-layouts  9.4 us
    pallas_call x1, Pallas kernels, on_device(): pl.pallas_call(functools.partial(halo_kernel, chunks), out_shape=(block,...  7.42 us

profile of v1, /device:TPU:0, one launch (start us, length us, event | category | flops | bytes accessed | tf_op | source)
XLA Modules:
  0.0 64.3 jit_solution(10743383256717262990)
XLA Ops:
  0.6 0.0 copy-start
  0.6 1.2 %copy-done = bf16[1,128,4096]{2,1,0:T(8,128)(2,1)S(1)} copy-done((bf16[1,128,4096]{2,1,0:T(8,128)(2,1)S(1)}, bf16[1,128,4096]{2,1,0:T(8,128)(2,1)}, u32[]{:S(2)}) %copy-start) | copy-done | bytes 1048600
  1.9 0.0 copy-start.2
  1.9 1.2 %copy-done.2 = bf16[1,128,4096]{2,1,0:T(8,128)(2,1)S(1)} copy-done((bf16[1,128,4096]{2,1,0:T(8,128)(2,1)S(1)}, bf16[1,128,4096]{2,1,0:T(8,128)(2,1)}, u32[]{:S(2)}) %copy-start.2) | copy-done | bytes 1048600
  3.1 0.0 copy-start.4
  3.1 1.2 %copy-done.4 = bf16[1,128,4096]{2,1,0:T(8,128)(2,1)S(1)} copy-done((bf16[1,128,4096]{2,1,0:T(8,128)(2,1)S(1)}, bf16[1,128,4096]{2,1,0:T(8,128)(2,1)}, u32[]{:S(2)}) %copy-start.4) | copy-done | bytes 1048600
  4.3 0.0 copy-start.10
  4.3 0.0 copy-start.1
  4.3 0.0 copy-start.3
  4.3 0.0 copy-start.5
  4.3 7.4 %halo.1 = (bf16[128,4096]{1,0:T(8,128)(2,1)S(1)}, bf16[128,4096]{1,0:T(8,128)(2,1)S(1)}) custom-call(bf16[128,4096]{1,0:T(8,128)(2,1)S(1)} %bitcast.10, bf16[128,4096]{1,0:T(8,128)(2,1)S(1)} %bitcast.12, bf16[128,4096]{1,0:T(8,128)(2,1)S(1)} %bitcast.14, bf16[128,4096]{1,0:T(8,128)(2,1)} %bitcast.16), custom_call_target="tpu_custom_call" | custom-call | tf_op jit(solution)/shard_map/halo/pallas_call | solution.py:254
  11.7 0.0 copy-start.7
  11.8 1.0 %copy-done.7 = bf16[128,4096]{1,0:T(8,128)(2,1)} copy-done((bf16[128,4096]{1,0:T(8,128)(2,1)}, bf16[128,4096]{1,0:T(8,128)(2,1)S(1)}, u32[]{:S(2)}) %copy-start.7) | copy-done | bytes 1048600
  12.7 0.0 copy-start.9
  12.7 1.0 %copy-done.9 = bf16[128,4096]{1,0:T(8,128)(2,1)} copy-done((bf16[128,4096]{1,0:T(8,128)(2,1)}, bf16[128,4096]{1,0:T(8,128)(2,1)S(1)}, u32[]{:S(2)}) %copy-start.9) | copy-done | bytes 1048600
  13.7 0.0 copy-done.10
  13.7 0.2 rev.6
  13.9 0.1 pad_convert_fusion.lines
  14.0 0.0 copy-done.1
  14.0 0.0 copy-done.3
  14.0 0.0 copy-done.5
  14.0 0.0 copy-start.6
  14.1 1.2 %copy-done.6 = bf16[1,128,4096]{2,1,0:T(8,128)(2,1)S(1)} copy-done((bf16[1,128,4096]{2,1,0:T(8,128)(2,1)S(1)}, bf16[1,128,4096]{2,1,0:T(8,128)(2,1)}, u32[]{:S(2)}) %copy-start.6) | copy-done | bytes 1048600
  15.3 0.0 copy-start.8
  15.3 1.2 %copy-done.8 = bf16[128,4096]{1,0:T(8,128)(2,1)S(1)} copy-done((bf16[128,4096]{1,0:T(8,128)(2,1)S(1)}, bf16[128,4096]{1,0:T(8,128)(2,1)}, u32[]{:S(2)}) %copy-start.8) | copy-done | bytes 1048600
  16.5 0.0 copy-start.11
  16.5 16.3 %mixer.1 = (bf16[128,4096]{1,0:T(8,128)(2,1)}, bf16[128,4096]{1,0:T(8,128)(2,1)}, bf16[128,4096]{1,0:T(8,128)(2,1)}, bf16[128,4096]{1,0:T(8,128)(2,1)}, f32[256,128]{1,0:T(8,128)S(1)}) custom-call(bf16[128,4096]{1,0:T(8,128)(2,1)S(1)} %bitcast.11, bf16[128,4096]{1,0:T(8,128)(2,1)S(1)} %bitcast.13, bf16[128,4096]{1,0:T(8,128)(2,1)S(1)} %bitcast.15, ...), custom_call_target="tpu_custom_call" | custom-call | tf_op jit(solution)/shard_map/mixer/pallas_call | solution.py:268
  32.8 0.0 copy-done.11
  32.8 0.1 rev.7
  32.8 30.1 %factors.1 = (f32[256,128]{1,0:T(8,128)S(1)}, f32[128,16]{1,0:T(8,128)S(1)}) custom-call(f32[32,8,128]{2,1,0:T(8,128)S(1)} %bitcast.18, f32[16,128]{1,0:T(8,128)S(1)} %bitcast.19), custom_call_target="tpu_custom_call" | custom-call | tf_op jit(solution)/shard_map/factors/pallas_call | solution.py:281
  63.0 0.7 %copy.12 = f32[128,16]{0,1:T(8,128)} copy(f32[128,16]{1,0:T(8,128)S(1)} %get-tuple-element.29) | data formatting | bytes 16384
  63.6 0.7 %copy.14 = f32[256,128]{1,0:T(8,128)} copy(f32[256,128]{1,0:T(8,128)S(1)} %get-tuple-element.40) | data formatting | bytes 262144
Async XLA Ops:
  0.6 1.2 %copy-start = (bf16[1,128,4096]{2,1,0:T(8,128)(2,1)S(1)}, bf16[1,128,4096]{2,1,0:T(8,128)(2,1)}, u32[]{:S(2)}) copy-start(bf16[1,128,4096]{2,1,0:T(8,128)(2,1)} %param.6) | copy-start | bytes 3145732
  1.9 1.2 %copy-start.2 = (bf16[1,128,4096]{2,1,0:T(8,128)(2,1)S(1)}, bf16[1,128,4096]{2,1,0:T(8,128)(2,1)}, u32[]{:S(2)}) copy-start(bf16[1,128,4096]{2,1,0:T(8,128)(2,1)} %param.7) | copy-start | bytes 3145732
  3.1 1.2 %copy-start.4 = (bf16[1,128,4096]{2,1,0:T(8,128)(2,1)S(1)}, bf16[1,128,4096]{2,1,0:T(8,128)(2,1)}, u32[]{:S(2)}) copy-start(bf16[1,128,4096]{2,1,0:T(8,128)(2,1)} %param.8) | copy-start | bytes 3145732
  4.3 9.4 %copy-start.10 = (bf16[256,128]{1,0:T(8,128)(2,1)S(1)}, bf16[256,128]{1,0:T(8,128)(2,1)}, u32[]{:S(2)}) copy-start(bf16[256,128]{1,0:T(8,128)(2,1)} %param.9) | copy-start | bytes 196612
  4.3 9.7 %copy-start.1 = (bf16[1,128,4096]{2,1,0:T(8,128)(2,1)S(1)}, bf16[1,128,4096]{2,1,0:T(8,128)(2,1)}, u32[]{:S(2)}) copy-start(bf16[1,128,4096]{2,1,0:T(8,128)(2,1)} %param.6) | copy-start | bytes 3145732
  4.3 9.7 %copy-start.3 = (bf16[1,128,4096]{2,1,0:T(8,128)(2,1)S(1)}, bf16[1,128,4096]{2,1,0:T(8,128)(2,1)}, u32[]{:S(2)}) copy-start(bf16[1,128,4096]{2,1,0:T(8,128)(2,1)} %param.7) | copy-start | bytes 3145732
  4.3 9.7 %copy-start.5 = (bf16[1,128,4096]{2,1,0:T(8,128)(2,1)S(1)}, bf16[1,128,4096]{2,1,0:T(8,128)(2,1)}, u32[]{:S(2)}) copy-start(bf16[1,128,4096]{2,1,0:T(8,128)(2,1)} %param.8) | copy-start | bytes 3145732
  11.7 1.0 %copy-start.7 = (bf16[128,4096]{1,0:T(8,128)(2,1)}, bf16[128,4096]{1,0:T(8,128)(2,1)S(1)}, u32[]{:S(2)}) copy-start(bf16[128,4096]{1,0:T(8,128)(2,1)S(1)} %get-tuple-element.15.prod_halo) | copy-start | bytes 3145732
  12.7 1.0 %copy-start.9 = (bf16[128,4096]{1,0:T(8,128)(2,1)}, bf16[128,4096]{1,0:T(8,128)(2,1)S(1)}, u32[]{:S(2)}) copy-start(bf16[128,4096]{1,0:T(8,128)(2,1)S(1)} %get-tuple-element.16.grad_halo) | copy-start | bytes 3145732
  14.0 1.2 %copy-start.6 = (bf16[1,128,4096]{2,1,0:T(8,128)(2,1)S(1)}, bf16[1,128,4096]{2,1,0:T(8,128)(2,1)}, u32[]{:S(2)}) copy-start(bf16[1,128,4096]{2,1,0:T(8,128)(2,1)} %param.10) | copy-start | bytes 3145732
  15.3 1.2 %copy-start.8 = (bf16[128,4096]{1,0:T(8,128)(2,1)S(1)}, bf16[128,4096]{1,0:T(8,128)(2,1)}, u32[]{:S(2)}) copy-start(bf16[128,4096]{1,0:T(8,128)(2,1)} %copy-done.7) | copy-start | bytes 3145732
  16.5 16.3 %copy-start.11 = (f32[128,16]{0,1:T(8,128)S(1)}, f32[128,16]{0,1:T(8,128)}, u32[]{:S(2)}) copy-start(f32[128,16]{0,1:T(8,128)} %param.11) | copy-start | bytes 24580

commit v2 on v0

v2 whole, which is shorter than its diff:
```python
import functools

import jax
import jax.numpy as jnp
from jax import lax
from jax.experimental import pallas as pl
from jax.experimental.pallas import tpu as pltpu
from jax.sharding import PartitionSpec as P

MESH = pl.DeviceIdType.MESH
HIGHEST = lax.Precision.HIGHEST
F32 = jnp.float32
BF16 = jnp.bfloat16
STEP = 32
LANES = 128
CHUNKS = 8
NT = (((1,), (1,)), ((), ()))
TN = (((0,), (0,)), ((), ()))


def flipped(size, dtype):
    rows = lax.broadcasted_iota(jnp.int32, (size, size), 0)
    cols = lax.broadcasted_iota(jnp.int32, (size, size), 1)
    return jnp.where(rows + cols == size - 1, 1.0, 0.0).astype(dtype)


def gated(left, right):
    return (left.astype(F32) * right.astype(F32)).astype(BF16)


def mixer_kernel(
    scale, q_in, k_in, v_in, g_in, filters, basis,
    mixed_out, grad_q_out, grad_k_out, grad_v_out, low_rank, basis_next,
    q, k, v, g, mixed, grad_q, grad_k, grad_v, ext_p, ext_g, bands, lag, parts, mine, gathered,
    load, store, send_p, recv_p, send_g, recv_g, send_a, recv_a, send_b, recv_b,
):
    dp, seq = lax.axis_size("dp"), lax.axis_size("seq")
    count = dp * seq
    pos = lax.axis_index("seq")
    last = seq - 1
    me = lax.axis_index("dp") * seq + pos
    tok, channels = q.shape
    groups, taps = filters.shape
    group = channels // groups
    per = LANES // group
    width = channels // CHUNKS
    subs = width // LANES
    blocks = tok // STEP
    rows = 2 * tok
    own = groups // count

    def chunk(c):
        return pl.ds(pl.multiple_of(c * width, width), width)

    def loads(c):
        return [
            pltpu.make_async_copy(src.at[:, chunk(c)], dst.at[:, chunk(c)], load.at[c, i])
            for i, (src, dst) in enumerate(((k_in, k), (v_in, v), (g_in, g), (q_in, q)))
        ]

    def stores(c):
        pairs = ((mixed, mixed_out), (grad_q, grad_q_out), (grad_k, grad_k_out), (grad_v, grad_v_out))
        return [
            pltpu.make_async_copy(src.at[:, chunk(c)], dst.at[:, chunk(c)], store.at[c, i])
            for i, (src, dst) in enumerate(pairs)
        ]

    def where(j):
        peer = lax.rem(me + j, count)
        return peer, (peer // seq, lax.rem(peer, seq))

    def to_next(c):
        return pltpu.make_async_remote_copy(
            src_ref=ext_p.at[pl.ds(tok, tok), chunk(c)], dst_ref=ext_p.at[pl.ds(0, tok), chunk(c)],
            send_sem=send_p.at[c], recv_sem=recv_p.at[c], device_id={"seq": pos + 1}, device_id_type=MESH)

    def to_previous(c):
        return pltpu.make_async_remote_copy(
            src_ref=ext_g.at[pl.ds(tok, tok), chunk(c)], dst_ref=ext_g.at[pl.ds(0, tok), chunk(c)],
            send_sem=send_g.at[c], recv_sem=recv_g.at[c], device_id={"seq": pos - 1}, device_id_type=MESH)

    def scatter(j):
        peer, place = where(j)
        return pltpu.make_async_remote_copy(
            src_ref=lag.at[peer], dst_ref=parts.at[j], send_sem=send_a.at[j],
            recv_sem=recv_a.at[j], device_id=place, device_id_type=MESH)

    def gather(j):
        return pltpu.make_async_remote_copy(
            src_ref=mine, dst_ref=gathered.at[me], send_sem=send_b.at[j],
            recv_sem=recv_b.at[j], device_id=where(j)[1], device_id_type=MESH)

    def gathered_from(j):
        return pltpu.make_async_remote_copy(
            src_ref=mine, dst_ref=gathered.at[lax.rem(me + count - j, count)], send_sem=send_b.at[j],
            recv_sem=recv_b.at[j], device_id=where(j)[1], device_id_type=MESH)

    barrier = pltpu.get_barrier_semaphore()

    @pl.loop(1, count)
    def _(j):
        pl.semaphore_signal(barrier, inc=1, device_id=where(j)[1], device_id_type=MESH)

    @pl.loop(0, CHUNKS)
    def _(c):
        for copy in loads(c):
            copy.start()

    flip = flipped(tok, BF16)
    flip2 = jnp.concatenate([flip, flip], axis=1)
    flip_taps = flipped(taps, F32)
    zeros = jnp.zeros((ext_p.shape[0] - rows, channels), BF16)
    ext_p[rows:, :] = zeros
    ext_g[rows:, :] = zeros

    @pl.when(pos == 0)
    def _():
        ext_p[0:tok, :] = jnp.zeros((tok, channels), BF16)

    @pl.when(pos == last)
    def _():
        ext_g[0:tok, :] = jnp.zeros((tok, channels), BF16)

    pl.semaphore_wait(barrier, count - 1)

    @pl.loop(0, CHUNKS)
    def _(c):
        for copy in loads(c):
            copy.wait()
        lanes = chunk(c)
        ext_p[pl.ds(tok, tok), lanes] = gated(k[:, lanes], v[:, lanes])
        ext_g[pl.ds(tok, tok), lanes] = jnp.dot(
            flip, gated(g[:, lanes], q[:, lanes]), preferred_element_type=F32).astype(BF16)

        @pl.when(pos < last)
        def _():
            to_next(c).start()

        @pl.when(pos > 0)
        def _():
            to_previous(c).start()

    @pl.loop(0, groups // per)
    def _(s):
        line = filters[pl.ds(pl.multiple_of(s * per, per), per), :].astype(F32)
        line = jnp.dot(line.astype(BF16), flip, preferred_element_type=F32)
        line = jnp.concatenate([line, jnp.zeros((per, rows - taps), F32)], axis=1)
        bands[s] = jnp.concatenate(
            [
                pltpu.roll(
                    jnp.broadcast_to(line[i : i + 1, :], (STEP, rows)), 1, axis=1, stride=1, stride_axis=0
                ).astype(BF16)
                for i in range(per)
            ],
            axis=0,
        )

    basis_rev = jnp.dot(basis[...], flip_taps, precision=HIGHEST, preferred_element_type=F32)
    owner = lax.broadcasted_iota(jnp.int32, (STEP, 2 * LANES), 1) % LANES // group

    def lag_sums(c):
        @pl.when(pos > 0)
        def _():
            to_next(c).wait_recv()

        for s in range(subs):
            lanes = pl.ds(pl.multiple_of(c * width + s * LANES, LANES), LANES)
            cross = jnp.zeros((per * STEP, rows), F32)
            for one in range(0, blocks, 2):
                two = one + 1
                at_one = tok + STEP * (blocks - 1 - one)
                at_two = tok + STEP * (blocks - 1 - two)
                cot = jnp.concatenate(
                    [ext_g[pl.ds(at_one, STEP), lanes], ext_g[pl.ds(at_two, STEP), lanes]], axis=1)
                windows = jnp.concatenate(
                    [ext_p[pl.ds(STEP * one, rows), lanes], ext_p[pl.ds(STEP * two, rows), lanes]], axis=1)
                masked = jnp.concatenate(
                    [jnp.where(owner == i, cot, jnp.zeros_like(cot)) for i in range(per)], axis=0)
                cross = cross + lax.dot_general(masked, windows, NT, preferred_element_type=F32)
            sums = []
            for i in range(per):
                skewed = pltpu.roll(
                    cross[i * STEP : (i + 1) * STEP, :], rows - STEP, axis=1, stride=1, stride_axis=0)
                sums.append(jnp.sum(skewed, axis=0, keepdims=True)[:, :tok])
            sums = jnp.concatenate(sums, axis=0).reshape(per // own, own, taps)
            lag[pl.ds((c * subs + s) * (per // own), per // own)] = sums

    def products(c):
        for s in range(subs):
            lanes = pl.ds(pl.multiple_of(c * width + s * LANES, LANES), LANES)
            band = bands[c * subs + s]
            found = []
            for a in range(blocks):
                window = jnp.concatenate(
                    [ext_p[pl.ds(STEP * a, rows), lanes], ext_g[pl.ds(STEP * a, rows), lanes]], axis=1)
                res = jnp.dot(band, window, preferred_element_type=F32)
                out = res[0:STEP, :]
                for i in range(1, per):
                    out = jnp.where(owner == i, res[i * STEP : (i + 1) * STEP, :], out)
                found.append(out)
            whole = jnp.concatenate(found, axis=0)
            conv = whole[:, :LANES]
            back = whole[:, LANES:]
            coarse = back.astype(BF16)
            fine = (back - coarse.astype(F32)).astype(BF16)
            grad_prod = jnp.dot(flip2, jnp.concatenate([coarse, fine], axis=0), preferred_element_type=F32)
            mixed[:, lanes] = (q[:, lanes].astype(F32) * conv).astype(BF16)
            grad_q[:, lanes] = (g[:, lanes].astype(F32) * conv).astype(BF16)
            grad_k[:, lanes] = (grad_prod * v[:, lanes].astype(F32)).astype(BF16)
            grad_v[:, lanes] = (grad_prod * k[:, lanes].astype(F32)).astype(BF16)
        for copy in stores(c):
            copy.start()

    @pl.loop(0, CHUNKS // 2)
    def _(h):
        for c in (2 * h, 2 * h + 1):
            lag_sums(c)

            @pl.when(pos < last)
            def _():
                to_previous(c).wait_recv()

        products(h)

    @pl.loop(1, count)
    def _(j):
        scatter(j).start()

    parts[0] = lag[me]

    @pl.loop(CHUNKS // 2, CHUNKS)
    def _(c):
        @pl.when(c == CHUNKS - CHUNKS // 4)
        def _():
            @pl.loop(1, count)
            def _(j):
                scatter(j).wait_recv()

            mine[...] = jnp.sum(parts[...], axis=0)

            @pl.loop(1, count)
            def _(j):
                gather(j).start()

        products(c)

    gathered[me] = mine[...]

    @pl.loop(1, count)
    def _(j):
        gathered_from(j).wait_recv()

    grads = gathered[...].reshape(groups, taps)
    left = lax.dot_general(basis_rev, grads, NT, precision=HIGHEST, preferred_element_type=F32)
    rank = left.shape[0]
    index = lax.broadcasted_iota(jnp.int32, left.shape, 0)
    rest = left
    ortho = jnp.zeros_like(left)
    for i in range(rank):
        column = rest[i : i + 1, :]
        norm = jnp.sum(column * column, axis=1, keepdims=True) + 1e-06
        along = jnp.sum(left * column, axis=1, keepdims=True)
        ortho = jnp.where(index == i, column / jnp.sqrt(norm), ortho)
        rest = rest - (along / norm) * column
    right = jnp.dot(ortho, grads, precision=HIGHEST, preferred_element_type=F32) * scale
    right = jnp.dot(right, flip_taps, precision=HIGHEST, preferred_element_type=F32)
    basis_next[...] = right
    low_rank[...] = lax.dot_general(ortho, right, TN, precision=HIGHEST, preferred_element_type=F32)

    @pl.loop(1, count)
    def _(j):
        scatter(j).wait_send()
        gather(j).wait_send()

    @pl.loop(0, CHUNKS)
    def _(c):
        for copy in stores(c):
            copy.wait()

        @pl.when(pos < last)
        def _():
            to_next(c).wait_send()

        @pl.when(pos > 0)
        def _():
            to_previous(c).wait_send()


def on_device(query_gate, key_gate, value_feat, filters, grad_out, basis_prev):
    q, k, v, g = query_gate[0], key_gate[0], value_feat[0], grad_out[0]
    tok, channels = q.shape
    groups, taps = filters.shape
    rank = basis_prev.shape[1]
    count = lax.axis_size("dp") * lax.axis_size("seq")
    scale = (count * tok * (channels // groups)) ** (-0.5)
    vmem = pl.BlockSpec(memory_space=pltpu.VMEM)
    anywhere = pl.BlockSpec(memory_space=pl.ANY)
    block = jax.ShapeDtypeStruct((tok, channels), BF16)
    held = pltpu.VMEM((tok, channels), BF16)
    padded = pltpu.VMEM((3 * tok - STEP, channels), BF16)
    per = LANES * groups // channels
    spread = pltpu.VMEM((count, groups // count, taps), F32)
    dma = pltpu.SemaphoreType.DMA
    mixed, grad_q, grad_k, grad_v, low_rank, basis_next = pl.pallas_call(
        functools.partial(mixer_kernel, scale),
        out_shape=(block,) * 4 + (
            jax.ShapeDtypeStruct((groups, taps), F32),
            jax.ShapeDtypeStruct((rank, taps), F32),
        ),
        in_specs=[anywhere] * 4 + [vmem] * 2,
        out_specs=[anywhere] * 4 + [vmem] * 2,
        scratch_shapes=[held] * 8 + [padded] * 2 + [
            pltpu.VMEM((groups // per, per * STEP, 2 * tok), BF16),
            spread, spread, pltpu.VMEM((groups // count, taps), F32), spread,
            dma((CHUNKS, 4)), dma((CHUNKS, 4)),
        ] + [dma((CHUNKS,))] * 4 + [dma((count,))] * 4,
        compiler_params=pltpu.CompilerParams(
            collective_id=0, has_side_effects=True, vmem_limit_bytes=56 * 2**20),
        name="mixer",
    )(q, k, v, g, filters, basis_prev.T)
    return (mixed[None], grad_q[None], grad_k[None], grad_v[None], low_rank, basis_next.T)


def solution(mesh):
    spec = P("dp", "seq", None)
    return jax.shard_map(
        on_device,
        mesh=mesh,
        in_specs=(spec, spec, spec, P(), spec, P()),
        out_specs=(spec, spec, spec, spec, P(), P()),
        check_vma=False,
    )
```

time: 464 us -> 52.8 us (0.11)
  local copies, waits for them, and re-layouts: 286 us -> 7.9 us
  waiting for transfers between devices: 53.1 us -> 0 us
  Pallas kernels: 0 us -> 43.9 us
  other arithmetic: 36.3 us -> 0 us
  matrix products: 28.7 us -> 0 us
  between operations: 26.1 us -> 0.66 us
  blocking collectives: 23.6 us -> 0 us
  starting transfers between devices: 5.35 us -> 0 us
    reshape x18 -> x0, local copies, waits for them, and re-layouts: 199 us -> none  [the longest x8 128 us: banded(): return tiled.reshape(count, rows, width)]
    psum x1 -> x0, waiting for transfers between devices: 53.1 us -> none  [on_device(): seq_grad = lax.psum(local_grad, 'seq')]
    slice x28 -> x0, local copies, waits for them, and re-layouts: 49.7 us -> none  [the longest x4 28.4 us: lag_sums(): flat = cross.reshape(count, rows * width)[:, :(rows - 1) * 2 * taps]]
    pallas_call x0 -> x1, Pallas kernels: none -> 43.9 us  [on_device(): pl.pallas_call(functools.partial(mixer_kernel, scale), out_shape=(block,)...]
    dot_general x43 -> x0, matrix products: 28.7 us -> none  [the longest x4 9.46 us: on_device(): jnp.einsum('gcu,gsu->gcs', prod_blk, forward_tab, preferred_element_type=...]
    unnamed x48 -> x16, local copies, waits for them, and re-layouts: 33.8 us -> 7.9 us
    psum x2 -> x0, blocking collectives: 23.6 us -> none  [the longest x1 16 us: on_device(): lax.psum(jnp.dot(seq_grad, basis_prev, precision=lax.Precision.HIGHEST),...]
    reduce_sum x20 -> x0, other arithmetic: 21.1 us -> none  [the longest x4 10.6 us: lag_sums(): upper = flat.reshape(count, rows - 1, 2 * taps)[:, :, :taps].sum(axis=1)]
  transfers between devices with their start and end apart: 3 -> 0, of which waited for: 1 -> 0; matrix products, arithmetic and copies ran while one was open for 38% -> 0% of each run, Pallas kernels for 0% -> 0%
where the time goes in v2:
time: 52.8 us; the launch traced here: 52.4 us
  Pallas kernels  43.9 us (83%)
  local copies, waits for them, and re-layouts  7.9 us (15%)
  between operations  0.66 us (1%)
    pallas_call x1, Pallas kernels, on_device(): pl.pallas_call(functools.partial(mixer_kernel, scale), out_shape=(block,)...  43.9 us
    unnamed x16, local copies, waits for them, and re-layouts  7.9 us

profile of v2, /device:TPU:0, one launch (start us, length us, event | category | flops | bytes accessed | tf_op | source)
XLA Modules:
  0.0 52.4 jit_solution(12257479844001659579)
XLA Ops:
  0.6 43.9 %mixer.1 = (bf16[128,4096]{1,0:T(8,128)(2,1)}, bf16[128,4096]{1,0:T(8,128)(2,1)}, bf16[128,4096]{1,0:T(8,128)(2,1)}, bf16[128,4096]{1,0:T(8,128)(2,1)}, f32[256,128]{1,0:T(8,128)}, /*index=5*/f32[16,128]{1,0:T(8,128)}) custom-call(bf16[128,4096]{1,0:T(8,128)(2,1)} %bitcast.14, bf16[128,4096]{1,0:T(8,128)(2,1)} %bitcast.15, bf16[128,4096]{1,0:T(8,128)(2,1)} %bitcast.16, ...), custom_call_target="tpu_custom_call" | custom-call | tf_op jit(solution)/shard_map/mixer/pallas_call | solution.py:304
  44.5 0.0 copy-start.2
  44.5 2.4 %copy.18 = bf16[1,128,4096]{2,1,0:T(8,128)(2,1)} copy(bf16[1,128,4096]{2,1,0:T(8,128)(2,1)} %bitcast.13) | data formatting | bytes 2097152
  46.9 0.0 copy-done.2
  46.9 0.0 copy-start.1
  46.9 1.0 %copy.19 = bf16[1,128,4096]{2,1,0:T(8,128)(2,1)} copy(bf16[1,128,4096]{2,1,0:T(8,128)(2,1)S(1)} %bitcast.12) | data formatting | bytes 2097152
  47.9 0.6 %copy-done.1 = bf16[128,4096]{1,0:T(8,128)(2,1)S(1)} copy-done((bf16[128,4096]{1,0:T(8,128)(2,1)S(1)}, bf16[128,4096]{1,0:T(8,128)(2,1)}, u32[]{:S(2)}) %copy-start.1) | copy-done | bytes 1048600
  48.5 0.0 copy-start
  48.5 1.0 %copy.20 = bf16[1,128,4096]{2,1,0:T(8,128)(2,1)} copy(bf16[1,128,4096]{2,1,0:T(8,128)(2,1)S(1)} %bitcast.11) | data formatting | bytes 2097152
  49.5 0.6 %copy-done = bf16[128,4096]{1,0:T(8,128)(2,1)S(1)} copy-done((bf16[128,4096]{1,0:T(8,128)(2,1)S(1)}, bf16[128,4096]{1,0:T(8,128)(2,1)}, u32[]{:S(2)}) %copy-start) | copy-done | bytes 1048600
  50.1 0.0 copy-start.3
  50.1 1.0 %copy.21 = bf16[1,128,4096]{2,1,0:T(8,128)(2,1)} copy(bf16[1,128,4096]{2,1,0:T(8,128)(2,1)S(1)} %bitcast.10) | data formatting | bytes 2097152
  51.1 0.1 copy-done.3
  51.1 0.0 copy-start.4
  51.1 0.7 %copy.22 = f32[256,128]{1,0:T(8,128)} copy(f32[256,128]{1,0:T(8,128)S(1)} %copy-done.3) | data formatting | bytes 262144
  51.8 0.0 copy-done.4
  51.8 0.6 %copy.23 = f32[128,16]{0,1:T(8,128)} copy(f32[128,16]{0,1:T(8,128)S(1)} %bitcast.19) | data formatting | bytes 16384
Async XLA Ops:
  44.5 2.4 %copy-start.2 = (bf16[128,4096]{1,0:T(8,128)(2,1)S(1)}, bf16[128,4096]{1,0:T(8,128)(2,1)}, u32[]{:S(2)}) copy-start(bf16[128,4096]{1,0:T(8,128)(2,1)} %get-tuple-element.13) | copy-start | bytes 3145732
  46.9 1.6 %copy-start.1 = (bf16[128,4096]{1,0:T(8,128)(2,1)S(1)}, bf16[128,4096]{1,0:T(8,128)(2,1)}, u32[]{:S(2)}) copy-start(bf16[128,4096]{1,0:T(8,128)(2,1)} %get-tuple-element.14) | copy-start | bytes 3145732
  48.5 1.6 %copy-start = (bf16[128,4096]{1,0:T(8,128)(2,1)S(1)}, bf16[128,4096]{1,0:T(8,128)(2,1)}, u32[]{:S(2)}) copy-start(bf16[128,4096]{1,0:T(8,128)(2,1)} %get-tuple-element.15) | copy-start | bytes 3145732
  50.1 1.0 %copy-start.3 = (f32[256,128]{1,0:T(8,128)S(1)}, f32[256,128]{1,0:T(8,128)}, u32[]{:S(2)}) copy-start(f32[256,128]{1,0:T(8,128)} %get-tuple-element.28) | copy-start | bytes 393220
  51.1 0.7 %copy-start.4 = (f32[16,128]{1,0:T(8,128)S(1)}, f32[16,128]{1,0:T(8,128)}, u32[]{:S(2)}) copy-start(f32[16,128]{1,0:T(8,128)} %get-tuple-element.17) | copy-start | bytes 24580

commit v3 on v2

--- a/solution.py
+++ b/solution.py
@@ -13,6 +13,7 @@
 BF16 = jnp.bfloat16
 STEP = 32
 LANES = 128
+PIECES = 4
 CHUNKS = 8
 NT = (((1,), (1,)), ((), ()))
 TN = (((0,), (0,)), ((), ()))
@@ -29,16 +30,15 @@
 
 
 def mixer_kernel(
-    scale, q_in, k_in, v_in, g_in, filters, basis,
-    mixed_out, grad_q_out, grad_k_out, grad_v_out, low_rank, basis_next,
-    q, k, v, g, mixed, grad_q, grad_k, grad_v, ext_p, ext_g, bands, lag, parts, mine, gathered,
-    load, store, send_p, recv_p, send_g, recv_g, send_a, recv_a, send_b, recv_b,
+    q_in, k_in, v_in, g_in, filters,
+    mixed_out, grad_q_out, grad_k_out, grad_v_out, gathered,
+    q, k, v, g, mixed, grad_q, grad_k, grad_v, ext_p, ext_g, bands, lag, parts, mine, shares, total,
+    load, store, send_p, recv_p, send_g, recv_g, stage_send, stage_recv,
 ):
     dp, seq = lax.axis_size("dp"), lax.axis_size("seq")
-    count = dp * seq
     pos = lax.axis_index("seq")
+    line_of = lax.axis_index("dp")
     last = seq - 1
-    me = lax.axis_index("dp") * seq + pos
     tok, channels = q.shape
     groups, taps = filters.shape
     group = channels // groups
@@ -47,7 +47,7 @@
     subs = width // LANES
     blocks = tok // STEP
     rows = 2 * tok
-    own = groups // count
+    units, unit = parts.shape[1:3]
 
     def chunk(c):
         return pl.ds(pl.multiple_of(c * width, width), width)
@@ -65,9 +65,11 @@
             for i, (src, dst) in enumerate(pairs)
         ]
 
-    def where(j):
-        peer = lax.rem(me + j, count)
-        return peer, (peer // seq, lax.rem(peer, seq))
+    def along_seq(j):
+        return lax.rem(pos + j, seq)
+
+    def along_dp(j):
+        return lax.rem(line_of + j, dp)
 
     def to_next(c):
         return pltpu.make_async_remote_copy(
@@ -80,35 +82,43 @@
             send_sem=send_g.at[c], recv_sem=recv_g.at[c], device_id={"seq": pos - 1}, device_id_type=MESH)
 
     def scatter(j):
-        peer, place = where(j)
-        return pltpu.make_async_remote_copy(
-            src_ref=lag.at[peer], dst_ref=parts.at[j], send_sem=send_a.at[j],
-            recv_sem=recv_a.at[j], device_id=place, device_id_type=MESH)
+        peer = along_seq(j)
+        return pltpu.make_async_remote_copy(
+            src_ref=lag.at[pl.ds(peer * units, units)], dst_ref=parts.at[j], send_sem=stage_send.at[0],
+            recv_sem=stage_recv.at[0], device_id={"seq": peer}, device_id_type=MESH)
+
+    def exchange(j):
+        return pltpu.make_async_remote_copy(
+            src_ref=mine, dst_ref=shares.at[line_of], send_sem=stage_send.at[1],
+            recv_sem=stage_recv.at[1], device_id={"dp": along_dp(j)}, device_id_type=MESH)
 
     def gather(j):
         return pltpu.make_async_remote_copy(
-            src_ref=mine, dst_ref=gathered.at[me], send_sem=send_b.at[j],
-            recv_sem=recv_b.at[j], device_id=where(j)[1], device_id_type=MESH)
-
-    def gathered_from(j):
-        return pltpu.make_async_remote_copy(
-            src_ref=mine, dst_ref=gathered.at[lax.rem(me + count - j, count)], send_sem=send_b.at[j],
-            recv_sem=recv_b.at[j], device_id=where(j)[1], device_id_type=MESH)
+            src_ref=total, dst_ref=gathered.at[pos], send_sem=stage_send.at[2],
+            recv_sem=stage_recv.at[2], device_id={"seq": along_seq(j)}, device_id_type=MESH)
+
+    def all_of(sems, stage):
+        size = shares if stage == 1 else parts
+        span = size.at[pl.ds(1, size.shape[0] - 1)]
+        pltpu.make_async_copy(span, span, sems.at[stage]).wait()
 
     barrier = pltpu.get_barrier_semaphore()
-
-    @pl.loop(1, count)
-    def _(j):
-        pl.semaphore_signal(barrier, inc=1, device_id=where(j)[1], device_id_type=MESH)
 
     @pl.loop(0, CHUNKS)
     def _(c):
         for copy in loads(c):
             copy.start()
 
+    @pl.loop(1, seq)
+    def _(j):
+        pl.semaphore_signal(barrier, inc=1, device_id={"seq": along_seq(j)}, device_id_type=MESH)
+
+    @pl.loop(1, dp)
+    def _(j):
+        pl.semaphore_signal(barrier, inc=1, device_id={"dp": along_dp(j)}, device_id_type=MESH)
+
     flip = flipped(tok, BF16)
     flip2 = jnp.concatenate([flip, flip], axis=1)
-    flip_taps = flipped(taps, F32)
     zeros = jnp.zeros((ext_p.shape[0] - rows, channels), BF16)
     ext_p[rows:, :] = zeros
     ext_g[rows:, :] = zeros
@@ -121,7 +131,7 @@
     def _():
         ext_g[0:tok, :] = jnp.zeros((tok, channels), BF16)
 
-    pl.semaphore_wait(barrier, count - 1)
+    pl.semaphore_wait(barrier, seq + dp - 2)
 
     @pl.loop(0, CHUNKS)
     def _(c):
@@ -155,7 +165,6 @@
             axis=0,
         )
 
-    basis_rev = jnp.dot(basis[...], flip_taps, precision=HIGHEST, preferred_element_type=F32)
     owner = lax.broadcasted_iota(jnp.int32, (STEP, 2 * LANES), 1) % LANES // group
 
     def lag_sums(c):
@@ -182,8 +191,8 @@
                 skewed = pltpu.roll(
                     cross[i * STEP : (i + 1) * STEP, :], rows - STEP, axis=1, stride=1, stride_axis=0)
                 sums.append(jnp.sum(skewed, axis=0, keepdims=True)[:, :tok])
-            sums = jnp.concatenate(sums, axis=0).reshape(per // own, own, taps)
-            lag[pl.ds((c * subs + s) * (per // own), per // own)] = sums
+            sums = jnp.concatenate(sums, axis=0).reshape(per // unit, unit, taps)
+            lag[pl.ds((c * subs + s) * (per // unit), per // unit)] = sums
 
     def products(c):
         for s in range(subs):
@@ -222,36 +231,76 @@
 
         products(h)
 
-    @pl.loop(1, count)
+    @pl.loop(1, seq)
     def _(j):
         scatter(j).start()
 
-    parts[0] = lag[me]
+    parts[0] = lag[pl.ds(pos * units, units)]
 
     @pl.loop(CHUNKS // 2, CHUNKS)
     def _(c):
-        @pl.when(c == CHUNKS - CHUNKS // 4)
-        def _():
-            @pl.loop(1, count)
+        @pl.when(c == CHUNKS - 2)
+        def _():
+            all_of(stage_recv, 0)
+            mine[...] = jnp.sum(parts[...], axis=0)
+
+            @pl.loop(1, dp)
             def _(j):
-                scatter(j).wait_recv()
-
-            mine[...] = jnp.sum(parts[...], axis=0)
-
-            @pl.loop(1, count)
+                exchange(j).start()
+
+            shares[line_of] = mine[...]
+
+        @pl.when(c == CHUNKS - 1)
+        def _():
+            all_of(stage_recv, 1)
+            total[...] = jnp.sum(shares[...], axis=0)
+
+            @pl.loop(1, seq)
             def _(j):
                 gather(j).start()
 
+            gathered[pos] = total[...]
+
         products(c)
 
-    gathered[me] = mine[...]
-
-    @pl.loop(1, count)
-    def _(j):
-        gathered_from(j).wait_recv()
-
-    grads = gathered[...].reshape(groups, taps)
-    left = lax.dot_general(basis_rev, grads, NT, precision=HIGHEST, preferred_element_type=F32)
+    all_of(stage_recv, 2)
+    for stage in range(3):
+        all_of(stage_send, stage)
+
+    @pl.loop(0, CHUNKS)
+    def _(c):
+        for copy in stores(c):
+            copy.wait()
+
+        @pl.when(pos < last)
+        def _():
+            to_next(c).wait_send()
+
+        @pl.when(pos > 0)
+        def _():
+            to_previous(c).wait_send()
+
+
+def factor_kernel(scale, grads, basis, *refs):
+    moved = tuple(zip(refs[:4], refs[4:8]))
+    low_rank, basis_next, sems = refs[8:]
+    tok = refs[0].shape[0]
+    piece = tok // PIECES
+
+    def moves():
+        return [
+            pltpu.make_async_copy(
+                src.at[pl.ds(p * piece, piece)], dst.at[pl.ds(p * piece, piece)], sems.at[i, p])
+            for i, (src, dst) in enumerate(moved)
+            for p in range(PIECES)
+        ]
+
+    for copy in moves():
+        copy.start()
+    taps = grads.shape[1]
+    flip_taps = flipped(taps, F32)
+    basis_rev = jnp.dot(basis[...], flip_taps, precision=HIGHEST, preferred_element_type=F32)
+    left = lax.dot_general(basis_rev, grads[...], NT, precision=HIGHEST, preferred_element_type=F32)
     rank = left.shape[0]
     index = lax.broadcasted_iota(jnp.int32, left.shape, 0)
     rest = left
@@ -262,28 +311,12 @@
         along = jnp.sum(left * column, axis=1, keepdims=True)
         ortho = jnp.where(index == i, column / jnp.sqrt(norm), ortho)
         rest = rest - (along / norm) * column
-    right = jnp.dot(ortho, grads, precision=HIGHEST, preferred_element_type=F32) * scale
+    right = jnp.dot(ortho, grads[...], precision=HIGHEST, preferred_element_type=F32) * scale
     right = jnp.dot(right, flip_taps, precision=HIGHEST, preferred_element_type=F32)
     basis_next[...] = right
     low_rank[...] = lax.dot_general(ortho, right, TN, precision=HIGHEST, preferred_element_type=F32)
-
-    @pl.loop(1, count)
-    def _(j):
-        scatter(j).wait_send()
-        gather(j).wait_send()
-
-    @pl.loop(0, CHUNKS)
-    def _(c):
-        for copy in stores(c):
-            copy.wait()
-
-        @pl.when(pos < last)
-        def _():
-            to_next(c).wait_send()
-
-        @pl.when(pos > 0)
-        def _():
-            to_previous(c).wait_send()
+    for copy in moves():
+        copy.wait()
 
 
 def on_device(query_gate, key_gate, value_feat, filters, grad_out, basis_prev):
@@ -291,33 +324,45 @@
     tok, channels = q.shape
     groups, taps = filters.shape
     rank = basis_prev.shape[1]
-    count = lax.axis_size("dp") * lax.axis_size("seq")
-    scale = (count * tok * (channels // groups)) ** (-0.5)
+    scale = (lax.axis_size("dp") * lax.axis_size("seq") * tok * (channels // groups)) ** (-0.5)
     vmem = pl.BlockSpec(memory_space=pltpu.VMEM)
     anywhere = pl.BlockSpec(memory_space=pl.ANY)
     block = jax.ShapeDtypeStruct((tok, channels), BF16)
     held = pltpu.VMEM((tok, channels), BF16)
     padded = pltpu.VMEM((3 * tok - STEP, channels), BF16)
     per = LANES * groups // channels
-    spread = pltpu.VMEM((count, groups // count, taps), F32)
+    dp, seq = lax.axis_size("dp"), lax.axis_size("seq")
+    unit = min(per, groups // seq)
+    share = (groups // seq // unit, unit, taps)
     dma = pltpu.SemaphoreType.DMA
+    *results, grads = pl.pallas_call(
+        mixer_kernel,
+        out_shape=(block,) * 4 + (jax.ShapeDtypeStruct((seq,) + share, F32),),
+        in_specs=[anywhere] * 4 + [vmem],
+        out_specs=[anywhere] * 4 + [vmem],
+        scratch_shapes=[held] * 8 + [padded] * 2 + [
+            pltpu.VMEM((groups // per, per * STEP, 2 * tok), BF16),
+            pltpu.VMEM((groups // unit, unit, taps), F32),
+            pltpu.VMEM((seq,) + share, F32), pltpu.VMEM(share, F32),
+            pltpu.VMEM((dp,) + share, F32), pltpu.VMEM(share, F32),
+            dma((CHUNKS, 4)), dma((CHUNKS, 4)),
+        ] + [dma((CHUNKS,))] * 4 + [dma((3,))] * 2,
+        compiler_params=pltpu.CompilerParams(
+            collective_id=0, has_side_effects=True, vmem_limit_bytes=56 * 2**20),
+        name="mixer",
+    )(q, k, v, g, filters)
     mixed, grad_q, grad_k, grad_v, low_rank, basis_next = pl.pallas_call(
-        functools.partial(mixer_kernel, scale),
+        functools.partial(factor_kernel, scale),
         out_shape=(block,) * 4 + (
             jax.ShapeDtypeStruct((groups, taps), F32),
             jax.ShapeDtypeStruct((rank, taps), F32),
         ),
-        in_specs=[anywhere] * 4 + [vmem] * 2,
+        in_specs=[vmem] * 2 + [anywhere] * 4,
         out_specs=[anywhere] * 4 + [vmem] * 2,
-        scratch_shapes=[held] * 8 + [padded] * 2 + [
-            pltpu.VMEM((groups // per, per * STEP, 2 * tok), BF16),
-            spread, spread, pltpu.VMEM((groups // count, taps), F32), spread,
-            dma((CHUNKS, 4)), dma((CHUNKS, 4)),
-        ] + [dma((CHUNKS,))] * 4 + [dma((count,))] * 4,
-        compiler_params=pltpu.CompilerParams(
-            collective_id=0, has_side_effects=True, vmem_limit_bytes=56 * 2**20),
-        name="mixer",
-    )(q, k, v, g, filters, basis_prev.T)
+        scratch_shapes=[dma((4, PIECES))],
+        compiler_params=pltpu.CompilerParams(vmem_limit_bytes=56 * 2**20),
+        name="factors",
+    )(grads.reshape(groups, taps), basis_prev.T, *results)
     return (mixed[None], grad_q[None], grad_k[None], grad_v[None], low_rank, basis_next.T)
 
 

time: 52.8 us -> 171 us (3.24)
  Pallas kernels: 43.9 us -> 170 us
  local copies, waits for them, and re-layouts: 7.9 us -> 0 us
    pallas_call x1 -> x2, Pallas kernels: 43.9 us -> 170 us  [the longest x1 130 us: on_device(): pl.pallas_call(functools.partial(factor_kernel, scale), out_shape=(block,...]
    unnamed x16 -> x0, local copies, waits for them, and re-layouts: 7.9 us -> none
where the time goes in v3:
time: 171 us
  Pallas kernels  170 us (99%)
    pallas_call x1, Pallas kernels, on_device(): pl.pallas_call(functools.partial(factor_kernel, scale), out_shape=(block,...  130 us
    pallas_call x1, Pallas kernels, on_device(): pl.pallas_call(mixer_kernel, out_shape=(block,) * 4 + (jax.ShapeDtypeStru...  40.3 us

profile of v3, /device:TPU:0, one launch (start us, length us, event | category | flops | bytes accessed | tf_op | source)
XLA Modules:
  0.0 170.8 jit_solution(9338927529928142441)
XLA Ops:
  0.6 40.3 %mixer.1 = (bf16[128,4096]{1,0:T(8,128)(2,1)}, bf16[128,4096]{1,0:T(8,128)(2,1)}, bf16[128,4096]{1,0:T(8,128)(2,1)}, bf16[128,4096]{1,0:T(8,128)(2,1)}, f32[8,4,8,128]{3,2,1,0:T(8,128)}) custom-call(bf16[128,4096]{1,0:T(8,128)(2,1)} %bitcast.11, bf16[128,4096]{1,0:T(8,128)(2,1)} %bitcast.12, bf16[128,4096]{1,0:T(8,128)(2,1)} %bitcast.13, ...), custom_call_target="tpu_custom_call" | custom-call | tf_op jit(solution)/shard_map/mixer/pallas_call | solution.py:338
  41.0 129.9 %factors.1 = (bf16[128,4096]{1,0:T(8,128)(2,1)}, bf16[128,4096]{1,0:T(8,128)(2,1)}, bf16[128,4096]{1,0:T(8,128)(2,1)}, bf16[128,4096]{1,0:T(8,128)(2,1)}, f32[256,128]{1,0:T(8,128)}, /*index=5*/f32[16,128]{1,0:T(8,128)}) custom-call(f32[256,128]{1,0:T(8,128)} %bitcast.15, f32[16,128]{1,0:T(8,128)} %bitcast.16, bf16[128,4096]{1,0:T(8,128)(2,1)} %get-tuple-element.18.refs_0_, ...), custom_call_target="tpu_custom_call" | custom-call | tf_op jit(solution)/shard_map/factors/pallas_call | solution.py:354

commit v4 on v3

--- a/solution.py
+++ b/solution.py
@@ -14,6 +14,7 @@
 STEP = 32
 LANES = 128
 PIECES = 4
+FLIGHT = 3
 CHUNKS = 8
 NT = (((1,), (1,)), ((), ()))
 TN = (((0,), (0,)), ((), ()))
@@ -131,10 +132,7 @@
     def _():
         ext_g[0:tok, :] = jnp.zeros((tok, channels), BF16)
 
-    pl.semaphore_wait(barrier, seq + dp - 2)
-
-    @pl.loop(0, CHUNKS)
-    def _(c):
+    def gates(c):
         for copy in loads(c):
             copy.wait()
         lanes = chunk(c)
@@ -142,6 +140,7 @@
         ext_g[pl.ds(tok, tok), lanes] = jnp.dot(
             flip, gated(g[:, lanes], q[:, lanes]), preferred_element_type=F32).astype(BF16)
 
+    def send(c):
         @pl.when(pos < last)
         def _():
             to_next(c).start()
@@ -149,6 +148,27 @@
         @pl.when(pos > 0)
         def _():
             to_previous(c).start()
+
+    def sent(c):
+        @pl.when(pos < last)
+        def _():
+            to_next(c).wait_send()
+
+        @pl.when(pos > 0)
+        def _():
+            to_previous(c).wait_send()
+
+    gates(0)
+    pl.semaphore_wait(barrier, seq + dp - 2)
+    send(0)
+
+    @pl.loop(1, CHUNKS)
+    def _(c):
+        gates(c)
+
+        @pl.when(c < FLIGHT)
+        def _():
+            send(c)
 
     @pl.loop(0, groups // per)
     def _(s):
@@ -223,6 +243,12 @@
     @pl.loop(0, CHUNKS // 2)
     def _(h):
         for c in (2 * h, 2 * h + 1):
+            sent(c)
+
+            @pl.when(c + FLIGHT < CHUNKS)
+            def _():
+                send(c + FLIGHT)
+
             lag_sums(c)
 
             @pl.when(pos < last)
@@ -272,30 +298,23 @@
         for copy in stores(c):
             copy.wait()
 
-        @pl.when(pos < last)
-        def _():
-            to_next(c).wait_send()
-
-        @pl.when(pos > 0)
-        def _():
-            to_previous(c).wait_send()
-
 
 def factor_kernel(scale, grads, basis, *refs):
     moved = tuple(zip(refs[:4], refs[4:8]))
-    low_rank, basis_next, sems = refs[8:]
-    tok = refs[0].shape[0]
-    piece = tok // PIECES
-
-    def moves():
-        return [
-            pltpu.make_async_copy(
-                src.at[pl.ds(p * piece, piece)], dst.at[pl.ds(p * piece, piece)], sems.at[i, p])
-            for i, (src, dst) in enumerate(moved)
-            for p in range(PIECES)
-        ]
-
-    for copy in moves():
+    low_rank, basis_next = refs[8:10]
+    held, sem_in, sem_out = refs[10:]
+    piece = refs[0].shape[0] // PIECES
+
+    def moves(inward):
+        copies = []
+        for i, (src, dst) in enumerate(moved):
+            for p in range(PIECES):
+                part = pl.ds(p * piece, piece)
+                ends = (src.at[part], held.at[i, part]) if inward else (held.at[i, part], dst.at[part])
+                copies.append(pltpu.make_async_copy(*ends, (sem_in if inward else sem_out).at[i, p]))
+        return copies
+
+    for copy in moves(True):
         copy.start()
     taps = grads.shape[1]
     flip_taps = flipped(taps, F32)
@@ -306,6 +325,10 @@
     rest = left
     ortho = jnp.zeros_like(left)
     for i in range(rank):
+        if i == 2:
+            for arrived, leaving in zip(moves(True), moves(False)):
+                arrived.wait()
+                leaving.start()
         column = rest[i : i + 1, :]
         norm = jnp.sum(column * column, axis=1, keepdims=True) + 1e-06
         along = jnp.sum(left * column, axis=1, keepdims=True)
@@ -315,7 +338,7 @@
     right = jnp.dot(right, flip_taps, precision=HIGHEST, preferred_element_type=F32)
     basis_next[...] = right
     low_rank[...] = lax.dot_general(ortho, right, TN, precision=HIGHEST, preferred_element_type=F32)
-    for copy in moves():
+    for copy in moves(False):
         copy.wait()
 
 
@@ -359,7 +382,7 @@
         ),
         in_specs=[vmem] * 2 + [anywhere] * 4,
         out_specs=[anywhere] * 4 + [vmem] * 2,
-        scratch_shapes=[dma((4, PIECES))],
+        scratch_shapes=[pltpu.VMEM((4, tok, channels), BF16), dma((4, PIECES)), dma((4, PIECES))],
         compiler_params=pltpu.CompilerParams(vmem_limit_bytes=56 * 2**20),
         name="factors",
     )(grads.reshape(groups, taps), basis_prev.T, *results)

time: 171 us -> 48 us (0.28)
  Pallas kernels: 170 us -> 47.1 us
    pallas_call x1, Pallas kernels: 130 us -> 6.69 us  [on_device(): pl.pallas_call(functools.partial(factor_kernel, scale), out_shape=(block,...]
where the time goes in v4:
time: 48 us; the launch traced here: 47.8 us
  Pallas kernels  47.1 us (98%)
  between operations  0.64 us (1%)
    pallas_call x1, Pallas kernels, on_device(): pl.pallas_call(mixer_kernel, out_shape=(block,) * 4 + (jax.ShapeDtypeStru...  40.4 us
    pallas_call x1, Pallas kernels, on_device(): pl.pallas_call(functools.partial(factor_kernel, scale), out_shape=(block,...  6.69 us

profile of v4, /device:TPU:0, one launch (start us, length us, event | category | flops | bytes accessed | tf_op | source)
XLA Modules:
  0.0 47.8 jit_solution(6914319059747307276)
XLA Ops:
  0.6 40.4 %mixer.1 = (bf16[128,4096]{1,0:T(8,128)(2,1)}, bf16[128,4096]{1,0:T(8,128)(2,1)}, bf16[128,4096]{1,0:T(8,128)(2,1)}, bf16[128,4096]{1,0:T(8,128)(2,1)}, f32[8,4,8,128]{3,2,1,0:T(8,128)}) custom-call(bf16[128,4096]{1,0:T(8,128)(2,1)} %bitcast.11, bf16[128,4096]{1,0:T(8,128)(2,1)} %bitcast.12, bf16[128,4096]{1,0:T(8,128)(2,1)} %bitcast.13, ...), custom_call_target="tpu_custom_call" | custom-call | tf_op jit(solution)/shard_map/mixer/pallas_call | solution.py:361
  41.1 6.7 %factors.1 = (bf16[128,4096]{1,0:T(8,128)(2,1)}, bf16[128,4096]{1,0:T(8,128)(2,1)}, bf16[128,4096]{1,0:T(8,128)(2,1)}, bf16[128,4096]{1,0:T(8,128)(2,1)}, f32[256,128]{1,0:T(8,128)}, /*index=5*/f32[16,128]{1,0:T(8,128)}) custom-call(f32[256,128]{1,0:T(8,128)} %bitcast.15, f32[16,128]{1,0:T(8,128)} %bitcast.16, bf16[128,4096]{1,0:T(8,128)(2,1)} %get-tuple-element.18.refs_0_, ...), custom_call_target="tpu_custom_call" | custom-call | tf_op jit(solution)/shard_map/factors/pallas_call | solution.py:377

commit v5 on v4

--- a/solution.py
+++ b/solution.py
@@ -33,7 +33,7 @@
 def mixer_kernel(
     q_in, k_in, v_in, g_in, filters,
     mixed_out, grad_q_out, grad_k_out, grad_v_out, gathered,
-    q, k, v, g, mixed, grad_q, grad_k, grad_v, ext_p, ext_g, bands, lag, parts, mine, shares, total,
+    q, k, v, g, mixed, grad_q, grad_k, grad_v, ext_p, ext_g, lines, lag, parts, mine, shares, total,
     load, store, send_p, recv_p, send_g, recv_g, stage_send, stage_recv,
 ):
     dp, seq = lax.axis_size("dp"), lax.axis_size("seq")
@@ -120,6 +120,8 @@
 
     flip = flipped(tok, BF16)
     flip2 = jnp.concatenate([flip, flip], axis=1)
+    lines[:, :taps] = jnp.dot(filters[...], flip, preferred_element_type=F32)
+    lines[:, taps:] = jnp.zeros((groups, rows - taps), F32)
     zeros = jnp.zeros((ext_p.shape[0] - rows, channels), BF16)
     ext_p[rows:, :] = zeros
     ext_g[rows:, :] = zeros
@@ -133,8 +135,6 @@
         ext_g[0:tok, :] = jnp.zeros((tok, channels), BF16)
 
     def gates(c):
-        for copy in loads(c):
-            copy.wait()
         lanes = chunk(c)
         ext_p[pl.ds(tok, tok), lanes] = gated(k[:, lanes], v[:, lanes])
         ext_g[pl.ds(tok, tok), lanes] = jnp.dot(
@@ -158,40 +158,21 @@
         def _():
             to_previous(c).wait_send()
 
-    gates(0)
-    pl.semaphore_wait(barrier, seq + dp - 2)
-    send(0)
-
-    @pl.loop(1, CHUNKS)
-    def _(c):
-        gates(c)
-
-        @pl.when(c < FLIGHT)
-        def _():
-            send(c)
-
-    @pl.loop(0, groups // per)
-    def _(s):
-        line = filters[pl.ds(pl.multiple_of(s * per, per), per), :].astype(F32)
-        line = jnp.dot(line.astype(BF16), flip, preferred_element_type=F32)
-        line = jnp.concatenate([line, jnp.zeros((per, rows - taps), F32)], axis=1)
-        bands[s] = jnp.concatenate(
-            [
-                pltpu.roll(
-                    jnp.broadcast_to(line[i : i + 1, :], (STEP, rows)), 1, axis=1, stride=1, stride_axis=0
-                ).astype(BF16)
-                for i in range(per)
-            ],
-            axis=0,
-        )
+    for low, high in ((0, 1), (1, FLIGHT), (FLIGHT, CHUNKS)):
+        for c in range(low, high):
+            for copy in loads(c):
+                copy.wait()
+        for c in range(low, high):
+            gates(c)
+        if low == 0:
+            pl.semaphore_wait(barrier, seq + dp - 2)
+        if low < FLIGHT:
+            for c in range(low, high):
+                send(c)
 
     owner = lax.broadcasted_iota(jnp.int32, (STEP, 2 * LANES), 1) % LANES // group
 
     def lag_sums(c):
-        @pl.when(pos > 0)
-        def _():
-            to_next(c).wait_recv()
-
         for s in range(subs):
             lanes = pl.ds(pl.multiple_of(c * width + s * LANES, LANES), LANES)
             cross = jnp.zeros((per * STEP, rows), F32)
@@ -217,7 +198,17 @@
     def products(c):
         for s in range(subs):
             lanes = pl.ds(pl.multiple_of(c * width + s * LANES, LANES), LANES)
-            band = bands[c * subs + s]
+            first = pl.multiple_of((c * subs + s) * per, per)
+            line = lines[pl.ds(first, per), :]
+            band = jnp.concatenate(
+                [
+                    pltpu.roll(
+                        jnp.broadcast_to(line[i : i + 1, :], (STEP, rows)), 1, axis=1, stride=1, stride_axis=0
+                    ).astype(BF16)
+                    for i in range(per)
+                ],
+                axis=0,
+            )
             found = []
             for a in range(blocks):
                 window = jnp.concatenate(
@@ -237,6 +228,7 @@
             grad_q[:, lanes] = (g[:, lanes].astype(F32) * conv).astype(BF16)
             grad_k[:, lanes] = (grad_prod * v[:, lanes].astype(F32)).astype(BF16)
             grad_v[:, lanes] = (grad_prod * k[:, lanes].astype(F32)).astype(BF16)
+    def store_all(c):
         for copy in stores(c):
             copy.start()
 
@@ -249,13 +241,18 @@
             def _():
                 send(c + FLIGHT)
 
-            lag_sums(c)
+            @pl.when(pos > 0)
+            def _():
+                to_next(c).wait_recv()
 
             @pl.when(pos < last)
             def _():
                 to_previous(c).wait_recv()
 
+        lag_sums(2 * h)
+        lag_sums(2 * h + 1)
         products(h)
+        store_all(h)
 
     @pl.loop(1, seq)
     def _(j):
@@ -263,9 +260,9 @@
 
     parts[0] = lag[pl.ds(pos * units, units)]
 
-    @pl.loop(CHUNKS // 2, CHUNKS)
-    def _(c):
-        @pl.when(c == CHUNKS - 2)
+    @pl.loop(0, 2)
+    def _(h):
+        @pl.when(h == 1)
         def _():
             all_of(stage_recv, 0)
             mine[...] = jnp.sum(parts[...], axis=0)
@@ -276,18 +273,20 @@
 
             shares[line_of] = mine[...]
 
-        @pl.when(c == CHUNKS - 1)
-        def _():
-            all_of(stage_recv, 1)
-            total[...] = jnp.sum(shares[...], axis=0)
-
-            @pl.loop(1, seq)
-            def _(j):
-                gather(j).start()
-
-            gathered[pos] = total[...]
-
-        products(c)
+        c = CHUNKS // 2 + h * (CHUNKS // 4)
+        for i in range(CHUNKS // 4):
+            products(c + i)
+        for i in range(CHUNKS // 4):
+            store_all(c + i)
+
+    all_of(stage_recv, 1)
+    total[...] = jnp.sum(shares[...], axis=0)
+
+    @pl.loop(1, seq)
+    def _(j):
+        gather(j).start()
+
+    gathered[pos] = total[...]
 
     all_of(stage_recv, 2)
     for stage in range(3):
@@ -364,7 +363,7 @@
         in_specs=[anywhere] * 4 + [vmem],
         out_specs=[anywhere] * 4 + [vmem],
         scratch_shapes=[held] * 8 + [padded] * 2 + [
-            pltpu.VMEM((groups // per, per * STEP, 2 * tok), BF16),
+            pltpu.VMEM((groups, 2 * tok), F32),
             pltpu.VMEM((groups // unit, unit, taps), F32),
             pltpu.VMEM((seq,) + share, F32), pltpu.VMEM(share, F32),
             pltpu.VMEM((dp,) + share, F32), pltpu.VMEM(share, F32),

time: 48 us -> 42.5 us (0.89)
  Pallas kernels: 47.1 us -> 41.7 us
    pallas_call x1, Pallas kernels: 40.4 us -> 35 us  [on_device(): pl.pallas_call(mixer_kernel, out_shape=(block,) * 4 + (jax.ShapeDtypeStru...]
where the time goes in v5:
time: 42.5 us; the launch traced here: 42.3 us
  Pallas kernels  41.7 us (98%)
  between operations  0.64 us (2%)
    pallas_call x1, Pallas kernels, on_device(): pl.pallas_call(mixer_kernel, out_shape=(block,) * 4 + (jax.ShapeDtypeStru...  35 us
    pallas_call x1, Pallas kernels, on_device(): pl.pallas_call(functools.partial(factor_kernel, scale), out_shape=(block,...  6.69 us

profile of v5, /device:TPU:0, one launch (start us, length us, event | category | flops | bytes accessed | tf_op | source)
XLA Modules:
  0.0 42.3 jit_solution(4165080018395825183)
XLA Ops:
  0.6 35.0 %mixer.1 = (bf16[128,4096]{1,0:T(8,128)(2,1)}, bf16[128,4096]{1,0:T(8,128)(2,1)}, bf16[128,4096]{1,0:T(8,128)(2,1)}, bf16[128,4096]{1,0:T(8,128)(2,1)}, f32[8,4,8,128]{3,2,1,0:T(8,128)}) custom-call(bf16[128,4096]{1,0:T(8,128)(2,1)} %bitcast.11, bf16[128,4096]{1,0:T(8,128)(2,1)} %bitcast.12, bf16[128,4096]{1,0:T(8,128)(2,1)} %bitcast.13, ...), custom_call_target="tpu_custom_call" | custom-call | tf_op jit(solution)/shard_map/mixer/pallas_call | solution.py:360
  35.6 6.7 %factors.1 = (bf16[128,4096]{1,0:T(8,128)(2,1)}, bf16[128,4096]{1,0:T(8,128)(2,1)}, bf16[128,4096]{1,0:T(8,128)(2,1)}, bf16[128,4096]{1,0:T(8,128)(2,1)}, f32[256,128]{1,0:T(8,128)}, /*index=5*/f32[16,128]{1,0:T(8,128)}) custom-call(f32[256,128]{1,0:T(8,128)} %bitcast.15, f32[16,128]{1,0:T(8,128)} %bitcast.16, bf16[128,4096]{1,0:T(8,128)(2,1)} %get-tuple-element.18.refs_0_, ...), custom_call_target="tpu_custom_call" | custom-call | tf_op jit(solution)/shard_map/factors/pallas_call | solution.py:376

commit v6 on v5

--- a/solution.py
+++ b/solution.py
@@ -14,7 +14,7 @@
 STEP = 32
 LANES = 128
 PIECES = 4
-FLIGHT = 3
+FLIGHT = 2
 CHUNKS = 8
 NT = (((1,), (1,)), ((), ()))
 TN = (((0,), (0,)), ((), ()))
@@ -195,10 +195,10 @@
             sums = jnp.concatenate(sums, axis=0).reshape(per // unit, unit, taps)
             lag[pl.ds((c * subs + s) * (per // unit), per // unit)] = sums
 
-    def products(c):
-        for s in range(subs):
-            lanes = pl.ds(pl.multiple_of(c * width + s * LANES, LANES), LANES)
-            first = pl.multiple_of((c * subs + s) * per, per)
+    def products(low, blocks_of):
+        for s in range(blocks_of):
+            lanes = pl.ds(pl.multiple_of((low + s) * LANES, LANES), LANES)
+            first = pl.multiple_of((low + s) * per, per)
             line = lines[pl.ds(first, per), :]
             band = jnp.concatenate(
                 [
@@ -251,7 +251,7 @@
 
         lag_sums(2 * h)
         lag_sums(2 * h + 1)
-        products(h)
+        products(h * subs, subs)
         store_all(h)
 
     @pl.loop(1, seq)
@@ -260,25 +260,21 @@
 
     parts[0] = lag[pl.ds(pos * units, units)]
 
-    @pl.loop(0, 2)
-    def _(h):
-        @pl.when(h == 1)
-        def _():
-            all_of(stage_recv, 0)
-            mine[...] = jnp.sum(parts[...], axis=0)
-
-            @pl.loop(1, dp)
-            def _(j):
-                exchange(j).start()
-
-            shares[line_of] = mine[...]
-
-        c = CHUNKS // 2 + h * (CHUNKS // 4)
-        for i in range(CHUNKS // 4):
-            products(c + i)
-        for i in range(CHUNKS // 4):
-            store_all(c + i)
-
+    left_over = (CHUNKS - CHUNKS // 2) * subs
+    third = left_over // 3
+    start = (CHUNKS // 2) * subs
+    products(start, left_over - 2 * third)
+    all_of(stage_recv, 0)
+    mine[...] = jnp.sum(parts[...], axis=0)
+
+    @pl.loop(1, dp)
+    def _(j):
+        exchange(j).start()
+
+    shares[line_of] = mine[...]
+    store_all(CHUNKS // 2)
+    start += left_over - 2 * third
+    products(start, third)
     all_of(stage_recv, 1)
     total[...] = jnp.sum(shares[...], axis=0)
 
@@ -287,6 +283,9 @@
         gather(j).start()
 
     gathered[pos] = total[...]
+    products(start + third, third)
+    for c in range(CHUNKS // 2 + 1, CHUNKS):
+        store_all(c)
 
     all_of(stage_recv, 2)
     for stage in range(3):

time: 42.5 us -> 43.5 us (1.024)
  Pallas kernels: 41.7 us -> 42.7 us
    pallas_call x1, Pallas kernels: 35 us -> 36 us  [on_device(): pl.pallas_call(mixer_kernel, out_shape=(block,) * 4 + (jax.ShapeDtypeStru...]
where the time goes in v6:
time: 43.5 us; the launch traced here: 43.4 us
  Pallas kernels  42.7 us (98%)
  between operations  0.64 us (1%)
    pallas_call x1, Pallas kernels, on_device(): pl.pallas_call(mixer_kernel, out_shape=(block,) * 4 + (jax.ShapeDtypeStru...  36 us
    pallas_call x1, Pallas kernels, on_device(): pl.pallas_call(functools.partial(factor_kernel, scale), out_shape=(block,...  6.69 us

profile of v6, /device:TPU:0, one launch (start us, length us, event | category | flops | bytes accessed | tf_op | source)
XLA Modules:
  0.0 43.4 jit_solution(11866453787075881776)
XLA Ops:
  0.6 36.0 %mixer.1 = (bf16[128,4096]{1,0:T(8,128)(2,1)}, bf16[128,4096]{1,0:T(8,128)(2,1)}, bf16[128,4096]{1,0:T(8,128)(2,1)}, bf16[128,4096]{1,0:T(8,128)(2,1)}, f32[8,4,8,128]{3,2,1,0:T(8,128)}) custom-call(bf16[128,4096]{1,0:T(8,128)(2,1)} %bitcast.11, bf16[128,4096]{1,0:T(8,128)(2,1)} %bitcast.12, bf16[128,4096]{1,0:T(8,128)(2,1)} %bitcast.13, ...), custom_call_target="tpu_custom_call" | custom-call | tf_op jit(solution)/shard_map/mixer/pallas_call | solution.py:359
  36.7 6.7 %factors.1 = (bf16[128,4096]{1,0:T(8,128)(2,1)}, bf16[128,4096]{1,0:T(8,128)(2,1)}, bf16[128,4096]{1,0:T(8,128)(2,1)}, bf16[128,4096]{1,0:T(8,128)(2,1)}, f32[256,128]{1,0:T(8,128)}, /*index=5*/f32[16,128]{1,0:T(8,128)}) custom-call(f32[256,128]{1,0:T(8,128)} %bitcast.15, f32[16,128]{1,0:T(8,128)} %bitcast.16, bf16[128,4096]{1,0:T(8,128)(2,1)} %get-tuple-element.18.refs_0_, ...), custom_call_target="tpu_custom_call" | custom-call | tf_op jit(solution)/shard_map/factors/pallas_call | solution.py:375

commit v7 on v6

--- a/solution.py
+++ b/solution.py
@@ -14,7 +14,6 @@
 STEP = 32
 LANES = 128
 PIECES = 4
-FLIGHT = 2
 CHUNKS = 8
 NT = (((1,), (1,)), ((), ()))
 TN = (((0,), (0,)), ((), ()))
@@ -158,7 +157,7 @@
         def _():
             to_previous(c).wait_send()
 
-    for low, high in ((0, 1), (1, FLIGHT), (FLIGHT, CHUNKS)):
+    for low, high in ((0, 1), (1, 3), (3, CHUNKS)):
         for c in range(low, high):
             for copy in loads(c):
                 copy.wait()
@@ -166,9 +165,8 @@
             gates(c)
         if low == 0:
             pl.semaphore_wait(barrier, seq + dp - 2)
-        if low < FLIGHT:
-            for c in range(low, high):
-                send(c)
+        for c in range(low, high):
+            send(c)
 
     owner = lax.broadcasted_iota(jnp.int32, (STEP, 2 * LANES), 1) % LANES // group
 
@@ -235,12 +233,6 @@
     @pl.loop(0, CHUNKS // 2)
     def _(h):
         for c in (2 * h, 2 * h + 1):
-            sent(c)
-
-            @pl.when(c + FLIGHT < CHUNKS)
-            def _():
-                send(c + FLIGHT)
-
             @pl.when(pos > 0)
             def _():
                 to_next(c).wait_recv()
@@ -293,6 +285,7 @@
 
     @pl.loop(0, CHUNKS)
     def _(c):
+        sent(c)
         for copy in stores(c):
             copy.wait()
 

time: 43.5 us -> 43 us (0.989)
  Pallas kernels: 42.7 us -> 42.2 us
    pallas_call x1, Pallas kernels: 36 us -> 35.5 us  [on_device(): pl.pallas_call(mixer_kernel, out_shape=(block,) * 4 + (jax.ShapeDtypeStru...]
where the time goes in v7:
time: 43 us; the launch traced here: 42.8 us
  Pallas kernels  42.2 us (98%)
  between operations  0.64 us (1%)
    pallas_call x1, Pallas kernels, on_device(): pl.pallas_call(mixer_kernel, out_shape=(block,) * 4 + (jax.ShapeDtypeStru...  35.5 us
    pallas_call x1, Pallas kernels, on_device(): pl.pallas_call(functools.partial(factor_kernel, scale), out_shape=(block,...  6.69 us

profile of v7, /device:TPU:0, one launch (start us, length us, event | category | flops | bytes accessed | tf_op | source)
XLA Modules:
  0.0 42.8 jit_solution(3002966415909277369)
XLA Ops:
  0.6 35.5 %mixer.1 = (bf16[128,4096]{1,0:T(8,128)(2,1)}, bf16[128,4096]{1,0:T(8,128)(2,1)}, bf16[128,4096]{1,0:T(8,128)(2,1)}, bf16[128,4096]{1,0:T(8,128)(2,1)}, f32[8,4,8,128]{3,2,1,0:T(8,128)}) custom-call(bf16[128,4096]{1,0:T(8,128)(2,1)} %bitcast.11, bf16[128,4096]{1,0:T(8,128)(2,1)} %bitcast.12, bf16[128,4096]{1,0:T(8,128)(2,1)} %bitcast.13, ...), custom_call_target="tpu_custom_call" | custom-call | tf_op jit(solution)/shard_map/mixer/pallas_call | solution.py:352
  36.1 6.7 %factors.1 = (bf16[128,4096]{1,0:T(8,128)(2,1)}, bf16[128,4096]{1,0:T(8,128)(2,1)}, bf16[128,4096]{1,0:T(8,128)(2,1)}, bf16[128,4096]{1,0:T(8,128)(2,1)}, f32[256,128]{1,0:T(8,128)}, /*index=5*/f32[16,128]{1,0:T(8,128)}) custom-call(f32[256,128]{1,0:T(8,128)} %bitcast.15, f32[16,128]{1,0:T(8,128)} %bitcast.16, bf16[128,4096]{1,0:T(8,128)(2,1)} %get-tuple-element.18.refs_0_, ...), custom_call_target="tpu_custom_call" | custom-call | tf_op jit(solution)/shard_map/factors/pallas_call | solution.py:368
